TPU v7x, 32 devices: a whole 2x2x4 slice. The times are simulated.
32 devices in a mesh: ens: 2 (over x), lat: 16 (over z, y, core).
Axes of the slice: x: 2, y: 2, z: 4, core: 2. Of those that a mesh axis runs over, the one named last changes fastest.
Arguments:
- atmos: bfloat16 [11520, 1024], P(('ens', 'lat')), parts along dimension 0, may hold values from -6 to 6
- ocean_state: bfloat16 [76, 128, 1440], P(None, ('ens', 'lat')), parts along dimension 1, may hold values from -6 to 6
- land_mask: int32 [64, 1440], P('lat'), may hold values 0 or 1
- w_qkv: bfloat16 [1024, 3072], replicated, may hold values from -0.1875 to 0.1875
- w_out: bfloat16 [1024, 1024], replicated, may hold values from -0.1875 to 0.1875
- head_scale: float32 [16], replicated, may hold values from 0.5 to 80
- gain_attn: float32 [1024], replicated, may hold values from 0.5 to 1.5
- gain_flux: float32 [1024], replicated, may hold values from 0.1 to 1.9
- w_flux: bfloat16 [1024, 16], replicated, may hold values from -0.1875 to 0.1875
- surf_embed: float32 [4, 1024], replicated, may hold values from -3 to 3
- flux_start: int32 [64], P('lat'), may hold values from 0 to 14, as said below
- flux_weight: float32 [64, 2], P('lat'), may hold values from 0.25 to 1
- surf_start: int32 [16], P('lat'), may hold values from -2 to 59, as said below
- surf_weight: float32 [16, 7], P('lat'), may hold values from 0.1 to 0.5
- conv_first: bfloat16 [9, 128, 92], replicated, may hold values from -0.21875 to 0.21875
- conv_second: bfloat16 [9, 76, 128], replicated, may hold values from -0.1875 to 0.1875
Outputs:
- atmos_next: bfloat16 [11520, 1024], P(('ens', 'lat')), parts along dimension 0
- ocean_next: bfloat16 [76, 128, 1440], P(None, ('ens', 'lat')), parts along dimension 1
There are 2 independent parts, one for each index of `ens`. A program takes and returns all parts, laid end to end along the dimension named above; an argument that names none is the same for every part. Nothing has to cross between parts.
Inputs may be any that keep to these rules, and one draw needn't show every extreme that they name: flux_start[i] is i // 4 - 1 or i // 4, kept within 0 to 14. surf_start[r] is 4 r - 2 or 4 r - 1.
All inputs are finite; a program needn't handle non-finite values. No bound on the sum of `land_mask` on one device may be relied on, other than what follows from the above.
Results may differ from a plain program's by a relative error of at most 0.0065.
The roundings to bfloat16 on the way count: a program that leaves them out, or rounds other values in their place, can miss the bound.
Values may be sent and summed in bfloat16 or wider, within the bound.
No kernel may reach another device: no remote copies, remote signals or barrier semaphores. Data moves between devices by JAX's collectives and lax.ppermute only.
A program may use at most 128 MiB of HBM per device.

v0:
```python
import functools

import jax
import jax.numpy as jnp
from jax import lax
from jax.experimental import pallas as pl
from jax.experimental.pallas import tpu as pltpu
from jax.sharding import PartitionSpec as P

LEVELS = 19
VARS = 4
SPAN = 4
PSIDE = 1024
WIDE = 256
LANE = 128
F32 = jnp.float32
BF16 = jnp.bfloat16
VMEM = pl.BlockSpec(memory_space=pltpu.VMEM)
SMEM = pl.BlockSpec(memory_space=pltpu.SMEM)


def limit(mebibytes):
    return pltpu.CompilerParams(vmem_limit_bytes=mebibytes * 2**20)


def cost(flops, size):
    return pl.CostEstimate(flops=int(flops), bytes_accessed=int(size), transcendentals=0)


def up_to(value, unit):
    return (value + unit - 1) // unit * unit


def iota(shape, axis):
    return lax.broadcasted_iota(jnp.int32, shape, axis)


def swap_in_chip(block):
    count = lax.axis_size("lat")
    return lax.ppermute(block, "lat", [(i, i ^ 1) for i in range(count)])


def swap_across(block):
    count = lax.axis_size("lat")
    pairs = []
    for i in range(1, count - 1, 2):
        pairs += [(i, i + 1), (i + 1, i)]
    return lax.ppermute(block, "lat", pairs)


def split3(values):
    high = values.astype(BF16)
    rest = values - high.astype(F32)
    middle = rest.astype(BF16)
    low = (rest - middle.astype(F32)).astype(BF16)
    return high, middle, low


def surface_kernel(pos_ref, small_ref, ocean_ref, out_ref, tile, *refs):
    fields, sems = refs
    orows, olon = fields.shape[1:]
    copies = [
        pltpu.make_async_copy(ocean_ref.at[v * LEVELS], fields.at[v], sems.at[v])
        for v in range(VARS)
    ]
    for copy in copies:
        copy.start()
    for copy in copies:
        copy.wait()
    wide = SPAN * LANE
    parts = jnp.concatenate([fields[v].astype(F32) for v in range(VARS)], axis=0).astype(BF16)
    gather = jnp.where(iota((wide, LANE), 0) // SPAN == iota((wide, LANE), 1), 1.0 / SPAN, 0.0)
    gather = gather.astype(BF16)
    tile[...] = jnp.zeros_like(tile)
    for at in range(0, olon, wide):
        size = min(wide, olon - at)
        tile[0:16, at // SPAN : at // SPAN + LANE] = jnp.dot(
            parts[:, at : at + size], gather[:size], preferred_element_type=F32
        )
    lanes = small_ref.shape[1]
    weights = lanes - 1 - orows - 2 * orows
    small = small_ref[...]
    for index, piece in enumerate(split3(small[:, 0:weights])):
        tile[16 + index : 17 + index, 0:weights] = piece.astype(F32)
    position = pos_ref[0].astype(F32)
    for band in range(2):
        at = weights + band * orows
        for index, piece in enumerate(split3(small[:, at : at + orows])):
            row = 20 + 2 * index + band
            tile[row : row + 1, 0:orows] = piece.astype(F32)
    at = weights + 2 * orows
    tile[26:27, 0:orows] = small[:, at : at + orows] - position
    tile[19:20, 0:1] = small[:, at + orows : lanes] - position * orows
    tile[27:28, 0:LANE] = jnp.ones((1, LANE), F32)
    out_ref[...] = tile[...].astype(BF16)


def surface_message(pos, ocean_state, surf_start, surf_weight, flux_start, flux_weight):
    channels, orows, olon = ocean_state.shape
    width = up_to(olon // SPAN, LANE)
    small = jnp.concatenate(
        [
            surf_weight.reshape(-1),
            flux_weight.T.reshape(-1),
            flux_start.astype(F32),
            surf_start.astype(F32),
        ]
    ).reshape(1, -1)
    return pl.pallas_call(
        surface_kernel,
        out_shape=jax.ShapeDtypeStruct((32, width), BF16),
        in_specs=[SMEM, VMEM, pl.BlockSpec(memory_space=pl.ANY)],
        out_specs=VMEM,
        scratch_shapes=[
            pltpu.VMEM((32, width), F32),
            pltpu.VMEM((VARS, orows, olon), BF16),
            pltpu.SemaphoreType.DMA((VARS,)),
        ],
        compiler_params=limit(8),
        cost_estimate=cost(1e12, 1e9),
        name="surface",
    )(pos, small, ocean_state)


def relayout_kernel(ocean_ref, mask_ref, after_ref, out_ref, wide, row_ref):
    channels, orows, olon = ocean_ref.shape
    width = out_ref.shape[2]
    wide[...] = ocean_ref[...].astype(F32)
    row_ref[...] = jnp.zeros_like(row_ref)
    pad = width - olon
    lanes = iota((1, width), 1)
    for row in range(orows):
        row_ref[0:channels, 0:olon] = wide[:, row, :]
        row_ref[channels : channels + 1, 0:olon] = mask_ref[row : row + 1, :].astype(F32)
        values = row_ref[...]
        ahead = pltpu.roll(values, olon, 1)
        behind = pltpu.roll(values, pad, 1)
        values = jnp.where((lanes >= olon) & (lanes < olon + SPAN), ahead, values)
        values = jnp.where(lanes >= width - SPAN, behind, values)
        out_ref[row] = values.astype(BF16)


def relayout(ocean_state, land_mask, after):
    channels, orows, olon = ocean_state.shape
    width = up_to(olon + 2 * SPAN, LANE)
    deep = up_to(channels + 1, 16)
    return pl.pallas_call(
        relayout_kernel,
        out_shape=jax.ShapeDtypeStruct((orows, deep, width), BF16),
        in_specs=[VMEM, VMEM, pl.BlockSpec(memory_space=pl.ANY)],
        out_specs=VMEM,
        scratch_shapes=[pltpu.VMEM((channels, orows, olon), F32), pltpu.VMEM((deep, width), F32)],
        compiler_params=limit(16),
        cost_estimate=cost(1e12, 1e9),
        name="relayout",
    )(ocean_state, land_mask, after)


def head_norm(block):
    side = 256
    ones = jnp.where(iota((side, side), 0) // 64 == iota((side, side), 1) // 64, 1.0, 0.0)
    ones = ones.astype(BF16)
    out = []
    for at in range(0, block.shape[1], side):
        part = block[:, at : at + side]
        square = part * part
        high = square.astype(BF16)
        low = (square - high.astype(F32)).astype(BF16)
        total = jnp.dot(high, ones, preferred_element_type=F32)
        total = total + jnp.dot(low, ones, preferred_element_type=F32)
        out.append(part * lax.rsqrt(total * (1.0 / 64) + 1e-06))
    return jnp.concatenate(out, axis=1)


def tokens_start(atmos, embed, sfields, places, params, orows):
    starts = params[19:20, 0:1].astype(F32)
    weights = (
        params[16:17].astype(F32) + params[17:18].astype(F32) + params[18:19].astype(F32)
    )[:, 0:LANE]
    rows = iota((16, LANE), 0) % orows
    lanes = iota((16, LANE), 1)
    total = None
    for block, fields in zip(places, sfields):
        place = rows + block * orows - starts.astype(jnp.int32)
        coef = jnp.sum(jnp.where(lanes == place, weights, 0.0), axis=1, keepdims=True)
        term = coef * fields[0:16].astype(F32)
        total = term if total is None else total + term
    a = split3(total)
    rep = jnp.concatenate(
        [jnp.broadcast_to(embed[v : v + 1], (orows, embed.shape[1])) for v in range(VARS)], axis=0
    )
    b = split3(rep)
    left = jnp.concatenate([a[0], a[0], a[0], a[1], a[1], a[2]], axis=0)
    right = jnp.concatenate([b[0], b[1], b[2], b[0], b[1], b[0]], axis=0)
    added = lax.dot_general(left, right, (((0,), (0,)), ((), ())), preferred_element_type=F32)
    return atmos.astype(F32) + added[: atmos.shape[0]]


def project_kernel(with_query, orows, pos_ref, scale_ref, atmos_ref, m0, m1, m2, embed_ref, gain_ref, w_ref, after_ref, *refs):
    outs = refs
    width, columns = w_ref.shape
    depth = width // scale_ref.shape[0]
    side = min(PSIDE, width)
    toward = 1 - 2 * (pos_ref[0] % 2)
    start = tokens_start(
        atmos_ref[...],
        embed_ref[...],
        (m0[...], m1[...], m2[...]),
        (0, toward, -toward),
        m0[...],
        orows,
    )
    mean = jnp.mean(start * start, axis=1, keepdims=True)
    normed = (start * lax.rsqrt(mean + 1e-06) * gain_ref[...]).astype(BF16)
    if with_query:
        outs[0][...] = start
    for at in range(0 if with_query else width, columns, side):
        block = jnp.dot(normed, w_ref[:, at : at + side], preferred_element_type=F32)
        if at < 2 * width:
            block = head_norm(block)
        if at < width:
            heads = iota((1, side), 1) // depth
            scale = jnp.zeros((1, side), F32)
            for h in range(side // depth):
                scale = jnp.where(heads == h, scale_ref[at // depth + h], scale)
            outs[1][:, at : at + side] = (
                block * (scale / jnp.sqrt(jnp.float32(depth)))
            ).astype(BF16)
        else:
            outs[-1][:, at - width : at - width + side] = block.astype(BF16)


def project(pos, atmos, messages, surf_embed, gain, scale, w_qkv, orows, with_query, after):
    tokens, width = atmos.shape
    out_shape = (jax.ShapeDtypeStruct((tokens, 2 * width), BF16),)
    if with_query:
        out_shape = (
            jax.ShapeDtypeStruct((tokens, width), F32),
            jax.ShapeDtypeStruct((tokens, width), BF16),
        ) + out_shape
    return pl.pallas_call(
        functools.partial(project_kernel, with_query, orows),
        out_shape=out_shape,
        in_specs=[SMEM, SMEM] + [VMEM] * 7 + [pl.BlockSpec(memory_space=pl.ANY)],
        out_specs=(VMEM,) * len(out_shape),
        compiler_params=limit(20),
        cost_estimate=cost(1e12, 1e9),
        name="project",
    )(pos, scale, atmos, *messages, surf_embed, gain, w_qkv, after)


def score_part(query, lanes, per, parts):
    none = jnp.zeros_like(query)
    tops = sums = mixed = None
    for head in range(per):
        mine = jnp.where(lanes == head, query, none)
        scores = [
            lax.dot_general(mine, key, (((1,), (1,)), ((), ())), preferred_element_type=F32)
            for key, _ in parts
        ]
        top = functools.reduce(jnp.maximum, [jnp.max(s, axis=1, keepdims=True) for s in scores])
        raised = [jnp.exp(s - top) for s in scores]
        total = sum(jnp.sum(r, axis=1, keepdims=True) for r in raised)
        out = sum(
            jnp.dot(r.astype(BF16), value, preferred_element_type=F32)
            for r, (_, value) in zip(raised, parts)
        )
        if head == 0:
            shape = out.shape
            tops, sums = jnp.broadcast_to(top, shape), jnp.broadcast_to(total, shape)
            mixed = out
        else:
            tops = jnp.where(lanes == head, top, tops)
            sums = jnp.where(lanes == head, total, sums)
            mixed = jnp.where(lanes == head, out, mixed)
    return tops, sums, mixed


def near_kernel(heads, q_ref, kv0, kv1, top_ref, sum_ref, mix_ref):
    rows, width = q_ref.shape
    per = WIDE * heads // width
    lanes = iota((1, WIDE), 1) // (width // heads)

    def group(g, carry):
        part = pl.ds(pl.multiple_of(g * WIDE, WIDE), WIDE)
        there = pl.ds(pl.multiple_of(width + g * WIDE, WIDE), WIDE)
        parts = [(kv[:, part], kv[:, there]) for kv in (kv0, kv1)]
        tops, sums, mixed = score_part(q_ref[:, part], lanes, per, parts)
        top_ref[:, part] = tops
        sum_ref[:, part] = sums
        mix_ref[:, part] = mixed
        return carry

    lax.fori_loop(0, width // WIDE, group, 0)


def attend_near(query, kv0, kv1, head_count):
    shape = jax.ShapeDtypeStruct(query.shape, F32)
    return pl.pallas_call(
        functools.partial(near_kernel, head_count),
        out_shape=(shape,) * 3,
        in_specs=[VMEM] * 3,
        out_specs=(VMEM,) * 3,
        compiler_params=limit(16),
        cost_estimate=cost(1, 1),
        name="near",
    )(query, kv0, kv1)


def far_kernel(heads, message_ref, q_ref, kv_ref, top_ref, sum_ref, mix_ref, wo_ref, start_ref, gain_ref, wf_ref, next_ref, flux_ref, total):
    rows, width = q_ref.shape
    per = WIDE * heads // width
    lanes = iota((1, WIDE), 1) // (width // heads)
    penalty = jnp.where(message_ref[27:28, 0:1].astype(F32) > 0.5, 0.0, 1e30)
    total[...] = start_ref[...]

    def group(g, carry):
        part = pl.ds(pl.multiple_of(g * WIDE, WIDE), WIDE)
        there = pl.ds(pl.multiple_of(width + g * WIDE, WIDE), WIDE)
        tops, sums, mixed = score_part(
            q_ref[:, part], lanes, per, [(kv_ref[:, part], kv_ref[:, there])]
        )
        tops = tops - penalty
        top = jnp.maximum(tops, top_ref[:, part])
        here, before = jnp.exp(tops - top), jnp.exp(top_ref[:, part] - top)
        mixed = mixed * here + mix_ref[:, part] * before
        mixed = mixed / (sums * here + sum_ref[:, part] * before)
        total[...] += jnp.dot(mixed.astype(BF16), wo_ref[part], preferred_element_type=F32)
        return carry

    lax.fori_loop(0, width // WIDE, group, 0)
    after = total[...]
    next_ref[...] = after.astype(BF16)
    mean = jnp.mean(after * after, axis=1, keepdims=True)
    flux_in = (after * lax.rsqrt(mean + 1e-06) * gain_ref[...]).astype(BF16)
    flux = lax.dot_general(
        wf_ref[...], flux_in, (((1,), (1,)), ((), ())), preferred_element_type=F32
    )
    flux_ref[...] = jnp.zeros_like(flux_ref)
    flux_ref[:, 0:rows] = flux.astype(BF16)


def attend_far(message, query, kv, near, w_out, start, gain, w_flux, head_count):
    tokens, width = query.shape
    flux_count = w_flux.shape[0]
    flux_width = up_to(tokens, LANE)
    return pl.pallas_call(
        functools.partial(far_kernel, head_count),
        out_shape=(
            jax.ShapeDtypeStruct((tokens, width), BF16),
            jax.ShapeDtypeStruct((flux_count, flux_width), BF16),
        ),
        in_specs=[VMEM] * 10,
        out_specs=(VMEM, VMEM),
        scratch_shapes=[pltpu.VMEM((tokens, width), F32)],
        compiler_params=limit(20),
        cost_estimate=cost(1e12, 1e9),
        name="far",
    )(message, query, kv, *near, w_out, start, gain, w_flux)


def gate_kernel(value_ref, after_ref, out_ref):
    pass


def gate(value, after):
    anywhere = pl.BlockSpec(memory_space=pl.ANY)
    return pl.pallas_call(
        gate_kernel,
        out_shape=jax.ShapeDtypeStruct(value.shape, value.dtype),
        in_specs=[anywhere, anywhere],
        out_specs=anywhere,
        input_output_aliases={0: 0},
        compiler_params=limit(1),
        cost_estimate=cost(1, 1),
        name="gate",
    )(value, after)


def gelu(x):
    inner = x * (0.7978845608028654 + 0.035677408136300125 * (x * x))
    return 0.5 * x * (1.0 + jnp.tanh(inner))


def ocean_kernel(channels, count, pos_ref, x0, x1, x2, p0, p1, p2, f0, f1, fx, fy, c1_ref, c2_ref, next_ref, out_ref, next_hbm, zbuf, hbuf, state, masks, f_ref, w1_ref, w2_ref, w1t, turned, sem):
    copy = pltpu.make_async_copy(next_ref, next_hbm, sem)
    copy.start()
    orows, deep, width = x0.shape
    olon = out_ref.shape[2]
    nflux = f_ref.shape[1]
    fwidth = f_ref.shape[2]
    tokens = olon // SPAN
    position = pos_ref[0]
    odd = position % 2
    toward = 1 - 2 * odd
    high = 3 * deep + 3 * nflux
    hid = w1_ref.shape[0]

    f_ref[2] = f0[...]
    f_ref[2 + toward] = f1[...]
    f_ref[2 - toward] = fx[0]
    f_ref[2 - 2 * toward] = fx[1]
    f_ref[2 + 2 * toward] = fy[0]

    w1t[...] = jnp.zeros_like(w1t)
    w2_ref[...] = jnp.zeros_like(w2_ref)
    for tap in range(9):
        di, dl = tap // 3, tap % 3
        values = c1_ref[tap].astype(F32)
        at = di * high + dl * deep
        w1t[at : at + channels] = values[:channels]
        at = di * high + 3 * deep + dl * nflux
        w1t[at : at + nflux] = values[channels:]
        for k in range(2):
            at = (tap + 3 * k) * hid
            w2_ref[80 * k : 80 * k + channels, at : at + hid] = c2_ref[tap]
    w1_ref[...] = w1t[...].T.astype(BF16)

    def put_state(row, values):
        zbuf[row, 0:deep] = pltpu.roll(values, 1, 1).astype(BF16)
        zbuf[row, deep : 2 * deep] = values.astype(BF16)
        zbuf[row, 2 * deep : 3 * deep] = pltpu.roll(values, width - 1, 1).astype(BF16)

    blocks = (
        (x0, p0, orows),
        (x1, p1, 2 * orows * (1 - odd)),
        (x2, p2, 2 * orows * odd),
    )
    expand = jnp.where(
        iota((LANE, SPAN * LANE), 0) == iota((LANE, SPAN * LANE), 1) // SPAN, 1.0, 0.0
    ).astype(BF16)
    flane = iota((1, fwidth), 1)
    for x_ref, p_ref, base in blocks:
        block = base // orows
        for i in range(orows):
            row = base + i
            values = x_ref[i].astype(F32)
            put_state(row, values)
            state[row] = values[0:80]
            masks[pl.ds(row, 1)] = values[channels : channels + 1][None]
            first, second = (
                p_ref[20 + b : 21 + b, i : i + 1].astype(F32)
                + p_ref[22 + b : 23 + b, i : i + 1].astype(F32)
                + p_ref[24 + b : 25 + b, i : i + 1].astype(F32)
                for b in range(2)
            )
            begin = p_ref[26:27, i : i + 1].astype(F32)
            total = None
            for d in (-1, 0, 1):
                coef = jnp.where(begin == d, first, 0.0) + jnp.where(
                    begin + 1.0 == d, second, 0.0
                )
                term = coef * f_ref[block + 1 + d].astype(F32)
                total = term if total is None else total + term
            ahead = pltpu.roll(total, tokens, 1)
            behind = pltpu.roll(total, fwidth - tokens, 1)
            total = jnp.where(flane == tokens, ahead, total)
            total = jnp.where(flane == fwidth - 1, behind, total)
            total = total.astype(BF16)
            spread = jnp.concatenate(
                [
                    jnp.dot(total[:, at : at + LANE], expand, preferred_element_type=F32)
                    for at in range(0, fwidth, LANE)
                ],
                axis=1,
            )
            at = 3 * deep
            zbuf[row, at : at + nflux] = pltpu.roll(spread, 1, 1).astype(BF16)
            zbuf[row, at + nflux : at + 2 * nflux] = spread.astype(BF16)
            zbuf[row, at + 2 * nflux : at + 3 * nflux] = pltpu.roll(spread, width - 1, 1).astype(BF16)

    def hidden_row(row, zrow, slot):
        taps = zbuf[pl.ds(zrow, 3)].reshape(3 * high, width)
        values = gelu(jnp.dot(w1_ref[...], taps, preferred_element_type=F32))
        place = position * orows + row
        keep = (place >= 0) & (place < count * orows)
        values = values * jnp.where(keep, 1.0, 0.0).astype(F32)
        hbuf[slot, 0:hid] = pltpu.roll(values, 1, 1).astype(BF16)
        hbuf[slot, hid : 2 * hid] = values.astype(BF16)
        hbuf[slot, 2 * hid : 3 * hid] = pltpu.roll(values, width - 1, 1).astype(BF16)

    def pair_update(hrow, srow):
        taps = hbuf[pl.ds(hrow, 4)].reshape(4 * 3 * hid, width)
        both = jnp.dot(w2_ref[...], taps, preferred_element_type=F32)
        for k in range(2):
            state[srow + k] += masks[srow + k] * both[80 * k : 80 * k + 80]

    def first_hidden(j, carry):
        hidden_row(j - 3, j, j)
        return carry

    lax.fori_loop(0, orows + 6, first_hidden, 0, unroll=True)

    def first_state(k, carry):
        pair_update(2 * k, 2 * k + 2)
        for m in range(2):
            put_state(2 * k + 2 + m, jnp.concatenate(
                [state[2 * k + 2 + m], jnp.zeros((deep - 80, width), F32)], axis=0
            ) if deep > 80 else state[2 * k + 2 + m])
        return carry

    lax.fori_loop(0, (orows + 4) // 2, first_state, 0, unroll=True)

    def second_hidden(j, carry):
        hidden_row(j - 1, j + 2, j)
        return carry

    lax.fori_loop(0, orows + 2, second_hidden, 0, unroll=True)
    for k in range(orows // 2):
        pair_update(2 * k, 2 * k + orows)
    for i in range(orows):
        turned[:, i, :] = state[orows + i][0:channels, 0:olon]
    out_ref[...] = turned[...].astype(BF16)
    copy.wait()


def ocean(pos, xs, messages, flux, conv_first, conv_second, tokens, channels, olon, count):
    orows, deep, width = xs[0].shape
    hid = conv_second.shape[2]
    nflux, fwidth = flux[0].shape
    high = 3 * deep + 3 * nflux
    return pl.pallas_call(
        functools.partial(ocean_kernel, channels, count),
        out_shape=(
            jax.ShapeDtypeStruct((channels, orows, olon), BF16),
            jax.ShapeDtypeStruct(tokens.shape, tokens.dtype),
        ),
        in_specs=[SMEM] + [VMEM] * 13,
        out_specs=(VMEM, pl.BlockSpec(memory_space=pltpu.HBM)),
        scratch_shapes=[
            pltpu.VMEM((3 * orows, high, width), BF16),
            pltpu.VMEM((orows + 6, 3 * hid, width), BF16),
            pltpu.VMEM((3 * orows, 80, width), F32),
            pltpu.VMEM((3 * orows, 1, width), F32),
            pltpu.VMEM((5, nflux, fwidth), BF16),
            pltpu.VMEM((hid, 3 * high), BF16),
            pltpu.VMEM((160, 12 * hid), BF16),
            pltpu.VMEM((3 * high, hid), F32),
            pltpu.VMEM((channels, orows, olon), F32),
            pltpu.SemaphoreType.DMA,
        ],
        compiler_params=limit(44),
        cost_estimate=cost(2e10, 1e7),
        name="ocean",
    )(pos, *xs, *messages, *flux, conv_first, conv_second, tokens)


def local(
    atmos,
    ocean_state,
    land_mask,
    w_qkv,
    w_out,
    head_scale,
    gain_attn,
    gain_flux,
    w_flux,
    surf_embed,
    flux_start,
    flux_weight,
    surf_start,
    surf_weight,
    conv_first,
    conv_second,
):
    position = lax.axis_index("lat")
    count = lax.axis_size("lat")
    channels, orows, olon = ocean_state.shape
    width = atmos.shape[1]
    head_count = head_scale.shape[0]
    pos = position.reshape(1).astype(jnp.int32)

    own = surface_message(pos, ocean_state, surf_start, surf_weight, flux_start, flux_weight)
    partner = swap_in_chip(own)
    far = swap_across(jnp.stack([own, partner]))
    cross, cross2 = far[0], far[1]
    atmos_cross = swap_across(atmos)

    gain_a = gain_attn.reshape(1, width)
    start, query, kv_own = project(
        pos, atmos, (own, partner, cross), surf_embed, gain_a, head_scale, w_qkv, orows, True, own
    )
    kv_partner = swap_in_chip(kv_own)
    xs_own = relayout(ocean_state, land_mask, query)
    near = attend_near(query, kv_own, kv_partner, head_count)
    (kv_cross,) = project(
        pos,
        atmos_cross,
        (cross, own, cross2),
        surf_embed,
        gain_a,
        head_scale,
        w_qkv,
        orows,
        False,
        near[0],
    )
    xs_own = gate(xs_own, query)
    xs_partner = swap_in_chip(xs_own)
    xs_cross = swap_across(xs_own)
    atmos_next, flux = attend_far(
        cross,
        query,
        kv_cross,
        near,
        w_out,
        start,
        gain_flux.reshape(1, width),
        w_flux.T,
        head_count,
    )
    flux_partner = swap_in_chip(flux)
    flux_far = swap_across(jnp.stack([flux, flux_partner]))
    flux_far2 = swap_in_chip(flux_far)
    ocean_next, atmos_next = ocean(
        pos,
        (xs_own, xs_partner, xs_cross),
        (own, partner, cross),
        (flux, flux_partner, flux_far, flux_far2),
        conv_first.transpose(0, 2, 1),
        conv_second,
        atmos_next,
        channels,
        olon,
        count,
    )
    return atmos_next, ocean_next


def solution(mesh):
    in_specs = (
        P(("ens", "lat"), None),
        P(None, ("ens", "lat"), None),
        P("lat", None),
        P(),
        P(),
        P(),
        P(),
        P(),
        P(),
        P(),
        P("lat"),
        P("lat", None),
        P("lat"),
        P("lat", None),
        P(),
        P(),
    )
    out_specs = (P(("ens", "lat"), None), P(None, ("ens", "lat"), None))
    return jax.shard_map(local, mesh=mesh, in_specs=in_specs, out_specs=out_specs, check_vma=False)
```

profile of v0, /device:TPU:25, one launch (start us, length us, event | category | flops | bytes accessed | tf_op | source)
XLA Modules:
  0.0 82.9 jit_solution(3221191296906097625)
XLA Ops:
  1.3 0.7 convert_element_type.6
  1.9 0.8 reshape.24
  2.7 0.7 maximum_bitcast_fusion.small_ref
  3.4 1.2 %copy-done.11 = bf16[76,4,1440]{2,1,0:T(4,128)(2,1)S(1)} copy-done((bf16[76,4,1440]{2,1,0:T(4,128)(2,1)S(1)}, bf16[76,4,1440]{2,1,0:T(4,128)(2,1)}, u32[]{:S(2)}) %copy-start.11) | copy-done | bytes 875544
  4.6 0.3 surface.1.m0.after_ref.m1.p0
  4.9 0.0 copy-start.2
  4.9 0.7 collective-permute-start
  5.7 0.8 %collective-permute-done.m1.p1 = bf16[32,384]{1,0:T(8,128)(2,1)S(1)} collective-permute-done((bf16[32,384]{1,0:T(8,128)(2,1)S(1)}, bf16[32,384]{1,0:T(8,128)(2,1)S(1)}, u32[]{:S(2)}, u32[]{:S(2)}) %collective-permute-start) | collective-permute-done | bytes 24608 | tf_op jit(solution)/shard_map/ppermute | solution.py:40
  6.6 3.5 %collective-permute-start.1 = (bf16[2,32,384]{2,1,0:T(8,128)(2,1)S(1)}, bf16[2,32,384]{2,1,0:T(8,128)(2,1)S(1)}, u32[]{:S(2)}, u32[]{:S(2)}) collective-permute-start(bf16[2,32,384]{2,1,0:T(8,128)(2,1)S(1)} %pad_maximum_fusion), channel_id=1, source_target_pairs={{1,2},{2,1},{3,4},{4,3},{5,6},{6,5},{7,8},{8,7},{9,10},{10,9},{11,... | collective-permute-start | bytes 147464 | tf_op jit(solution)/shard_map/ppermute | solution.py:48
  10.1 2.1 %collective-permute-start.4 = (bf16[360,1024]{1,0:T(8,128)(2,1)}, bf16[360,1024]{1,0:T(8,128)(2,1)}, u32[]{:S(2)}, u32[]{:S(2)}) collective-permute-start(bf16[360,1024]{1,0:T(8,128)(2,1)} %atmos_ref.1), channel_id=1, source_target_pairs={{1,2},{2,1},{3,4},{4,3},{5,6},{6,5},{7,8},{8,7},{9,10},{10,9},{11,... | collective-permute-start | bytes 2211848 | tf_op jit(solution)/shard_map/ppermute | solution.py:48
  12.2 0.0 copy-start.12
  12.2 0.0 copy-start.16
  12.2 6.4 %project.2 = (f32[360,1024]{1,0:T(8,128)S(1)}, bf16[360,1024]{1,0:T(8,128)(2,1)S(1)}, bf16[360,2048]{1,0:T(8,128)(2,1)}) custom-call(s32[1]{0:T(128)} %bitcast.pos_ref, f32[16]{0:T(128)S(1)} %copy-done.20, bf16[360,1024]{1,0:T(8,128)(2,1)} %atmos_ref.1, bf16[32,384]{1,0:T(8,128)(2,1)S(1)} %surface.1.m0.after_ref.m1.p0, ...), custom_call_target="tpu_custom_call" | custom-call | flops 999999995904 | bytes 1000000000 | tf_op jit(solution)/shard_map/project/pallas_call | solution.py:241
  18.6 1.4 %collective-permute-start.5 = (bf16[360,2048]{1,0:T(8,128)(2,1)}, bf16[360,2048]{1,0:T(8,128)(2,1)}, u32[]{:S(2)}, u32[]{:S(2)}) collective-permute-start(bf16[360,2048]{1,0:T(8,128)(2,1)} %get-tuple-element.13.kv0), channel_id=1, source_target_pairs={{0,1},{1,0},{2,3},{3,2},{4,5},{5,4},{6,7},{7,6},{8,9},{9,8},{10,11... | collective-permute-start | bytes 4423688 | tf_op jit(solution)/shard_map/ppermute | solution.py:40
  20.1 1.6 %relayout.1.value_ref = bf16[4,80,1536]{2,1,0:T(8,128)(2,1)} custom-call(bf16[76,4,1440]{2,1,0:T(4,128)(2,1)S(1)} %copy-done.12, s32[4,1440]{1,0:T(4,128)S(1)} %copy-done.16, bf16[360,1024]{1,0:T(8,128)(2,1)S(1)} %get-tuple-element.12.after_ref.q_ref), custom_call_target="tpu_custom_call" | custom-call | flops 999999995904 | bytes 1000000000 | tf_op jit(solution)/shard_map/relayout/pallas_call | solution.py:147
  21.7 0.0 collective-permute-start.2
  21.8 2.9 %collective-permute-start.3 = (bf16[4,80,1536]{2,1,0:T(8,128)(2,1)}, bf16[4,80,1536]{2,1,0:T(8,128)(2,1)}, u32[]{:S(2)}, u32[]{:S(2)}) collective-permute-start(bf16[4,80,1536]{2,1,0:T(8,128)(2,1)} %gate.1.x0), channel_id=1, source_target_pairs={{1,2},{2,1},{3,4},{4,3},{5,6},{6,5},{7,8},{8,7},{9,10},{10,9},{11,... | collective-permute-start | bytes 2949128 | tf_op jit(solution)/shard_map/ppermute | solution.py:48
  24.6 11.9 %near.1 = (f32[360,1024]{1,0:T(8,128)S(1)}, f32[360,1024]{1,0:T(8,128)S(1)}, f32[360,1024]{1,0:T(8,128)S(1)}) custom-call(bf16[360,1024]{1,0:T(8,128)(2,1)S(1)} %get-tuple-element.12.after_ref.q_ref, bf16[360,2048]{1,0:T(8,128)(2,1)} %get-tuple-element.13.kv0, bf16[360,2048]{1,0:T(8,128)(2,1)} %collective-permute-done.5.kv1), custom_call_target="tpu_custom_call" | custom-call | flops 1 | bytes 1 | tf_op jit(solution)/shard_map/near/pallas_call | solution.py:299
  36.6 5.0 %collective-permute-done.4.atmos_ref = bf16[360,1024]{1,0:T(8,128)(2,1)} collective-permute-done((bf16[360,1024]{1,0:T(8,128)(2,1)}, bf16[360,1024]{1,0:T(8,128)(2,1)}, u32[]{:S(2)}, u32[]{:S(2)}) %collective-permute-start.4) | collective-permute-done | bytes 737312 | tf_op jit(solution)/shard_map/ppermute | solution.py:48
  41.6 0.0 copy-start.1
  41.6 0.0 copy-start.10
  41.6 0.0 copy-start.15
  41.7 0.0 copy-start.19
  41.7 4.0 %project.3.kv_ref = bf16[360,2048]{1,0:T(8,128)(2,1)S(1)} custom-call(s32[1]{0:T(128)} %bitcast.pos_ref, f32[16]{0:T(128)S(1)} %copy-done.20, bf16[360,1024]{1,0:T(8,128)(2,1)} %collective-permute-done.4.atmos_ref, bf16[32,384]{1,0:T(8,128)(2,1)S(1)} %copy-done.7, bf16[32,384]{1,0:T(8,128)(2,1)S(1)} %surface.1.m0.after_ref.m1.p0, ...), custom_call_target="tpu_custom_call" | custom-call | flops 999999995904 | bytes 1000000000 | tf_op jit(solution)/shard_map/project/pallas_call | solution.py:241
  45.8 0.0 copy-start.14
  45.8 7.3 %far.1 = (bf16[360,1024]{1,0:T(8,128)(2,1)S(1)}, bf16[16,384]{1,0:T(8,128)(2,1)S(1)}) custom-call(bf16[32,384]{1,0:T(8,128)(2,1)S(1)} %copy-done.7, bf16[360,1024]{1,0:T(8,128)(2,1)S(1)} %copy-done.1, bf16[360,2048]{1,0:T(8,128)(2,1)S(1)} %project.3.kv_ref, f32[360,1024]{1,0:T(8,128)S(1)} %get-tuple-element.14.after_ref.top_ref, ...), custom_call_target="tpu_custom_call" | custom-call | flops 999999995904 | bytes 1000000000 | tf_op jit(solution)/shard_map/far/pallas_call | solution.py:347
  53.1 1.2 %collective-permute-done.6.f1 = bf16[16,384]{1,0:T(8,128)(2,1)S(1)} collective-permute-done((bf16[16,384]{1,0:T(8,128)(2,1)S(1)}, bf16[16,384]{1,0:T(8,128)(2,1)S(1)}, u32[]{:S(2)}, u32[]{:S(2)}) %collective-permute-start.6) | collective-permute-done | bytes 12320 | tf_op jit(solution)/shard_map/ppermute | solution.py:40
  54.3 2.1 %collective-permute-start.7 = (bf16[2,16,384]{2,1,0:T(8,128)(2,1)S(1)}, bf16[2,16,384]{2,1,0:T(8,128)(2,1)S(1)}, u32[]{:S(2)}, u32[]{:S(2)}) collective-permute-start(bf16[2,16,384]{2,1,0:T(8,128)(2,1)S(1)} %pad_maximum_fusion.1), channel_id=1, source_target_pairs={{1,2},{2,1},{3,4},{4,3},{5,6},{6,5},{7,8},{8,7},{9,10},{10,9},{11,... | collective-permute-start | bytes 73736 | tf_op jit(solution)/shard_map/ppermute | solution.py:48
  56.4 3.3 %collective-permute-done.7.fx = bf16[2,16,384]{2,1,0:T(8,128)(2,1)S(1)} collective-permute-done((bf16[2,16,384]{2,1,0:T(8,128)(2,1)S(1)}, bf16[2,16,384]{2,1,0:T(8,128)(2,1)S(1)}, u32[]{:S(2)}, u32[]{:S(2)}) %collective-permute-start.7) | collective-permute-done | bytes 24608 | tf_op jit(solution)/shard_map/ppermute | solution.py:48
  59.7 0.8 collective-permute-start.8
  60.5 0.8 %collective-permute-done.8.fy = bf16[2,16,384]{2,1,0:T(8,128)(2,1)S(1)} collective-permute-done((bf16[2,16,384]{2,1,0:T(8,128)(2,1)S(1)}, bf16[2,16,384]{2,1,0:T(8,128)(2,1)S(1)}, u32[]{:S(2)}, u32[]{:S(2)}) %collective-permute-start.8) | collective-permute-done | bytes 24608 | tf_op jit(solution)/shard_map/ppermute | solution.py:40
  61.4 21.3 %ocean.1 = (bf16[76,4,1440]{2,1,0:T(4,128)(2,1)}, bf16[360,1024]{1,0:T(8,128)(2,1)}) custom-call(s32[1]{0:T(128)} %bitcast.pos_ref, bf16[4,80,1536]{2,1,0:T(8,128)(2,1)} %gate.1.x0, bf16[4,80,1536]{2,1,0:T(8,128)(2,1)} %collective-permute-done.2.x1, bf16[4,80,1536]{2,1,0:T(8,128)(2,1)} %collective-permute-done.3.x2, bf16[32,384]{1,0:T(8,128)(2,1)S(1)} %copy-done.3, ...), custom_call_target="tpu_custom_call" | custom-call | flops 20000000000 | bytes 10000000 | tf_op jit(solution)/shard_map/ocean/pallas_call | solution.py:522
  (42 shorter events, 0.1 us)
Async XLA Ops:
  3.4 1.2 %copy-start.11 = (bf16[76,4,1440]{2,1,0:T(4,128)(2,1)S(1)}, bf16[76,4,1440]{2,1,0:T(4,128)(2,1)}, u32[]{:S(2)}) copy-start(bf16[76,4,1440]{2,1,0:T(4,128)(2,1)} %ocean_ref.3) | copy-start | bytes 2626564
  4.6 7.6 %copy-start.8 = (bf16[1024,3072]{1,0:T(8,128)(2,1)S(1)}, bf16[1024,3072]{1,0:T(8,128)(2,1)}, u32[]{:S(2)}) copy-start(bf16[1024,3072]{1,0:T(8,128)(2,1)} %w_ref.3) | copy-start | bytes 18874372
  4.6 7.6 %copy-start.17 = (f32[4,1024]{1,0:T(4,128)S(1)}, f32[4,1024]{1,0:T(4,128)}, u32[]{:S(2)}) copy-start(f32[4,1024]{1,0:T(4,128)} %embed_ref.3) | copy-start | bytes 49156
  4.6 7.6 %copy-start.18 = (f32[1024]{0:T(1024)S(1)}, f32[1024]{0:T(1024)}, u32[]{:S(2)}) copy-start(f32[1024]{0:T(1024)} %param.22) | copy-start | bytes 12292
  4.6 7.6 %copy-start.20 = (f32[16]{0:T(128)S(1)}, f32[16]{0:T(128)}, u32[]{:S(2)}) copy-start(f32[16]{0:T(128)} %scale_ref.3) | copy-start | bytes 196
  4.9 36.7 %copy-start.2 = (bf16[32,384]{1,0:T(8,128)(2,1)}, bf16[32,384]{1,0:T(8,128)(2,1)S(1)}, u32[]{:S(2)}) copy-start(bf16[32,384]{1,0:T(8,128)(2,1)S(1)} %surface.1.m0.after_ref.m1.p0) | copy-start | bytes 73732
  4.9 1.6 %collective-permute-start = (bf16[32,384]{1,0:T(8,128)(2,1)S(1)}, bf16[32,384]{1,0:T(8,128)(2,1)S(1)}, u32[]{:S(2)}, u32[]{:S(2)}) collective-permute-start(bf16[32,384]{1,0:T(8,128)(2,1)S(1)} %surface.1.m0.after_ref.m1.p0), channel_id=1, source_target_pairs={{0,1},{1,0},{2,3},{3,2},{4,5},{5,4},{6,7},{7,6},{8,9},{9,8},{10,11... | collective-permute-start | bytes 73736 | tf_op jit(solution)/shard_map/ppermute | solution.py:40
  6.5 12.1 %copy-start.4 = (bf16[32,384]{1,0:T(8,128)(2,1)}, bf16[32,384]{1,0:T(8,128)(2,1)S(1)}, u32[]{:S(2)}) copy-start(bf16[32,384]{1,0:T(8,128)(2,1)S(1)} %collective-permute-done.m1.p1) | copy-start | bytes 73732
  6.6 5.6 %collective-permute-start.1 = (bf16[2,32,384]{2,1,0:T(8,128)(2,1)S(1)}, bf16[2,32,384]{2,1,0:T(8,128)(2,1)S(1)}, u32[]{:S(2)}, u32[]{:S(2)}) collective-permute-start(bf16[2,32,384]{2,1,0:T(8,128)(2,1)S(1)} %pad_maximum_fusion), channel_id=1, source_target_pairs={{1,2},{2,1},{3,4},{4,3},{5,6},{6,5},{7,8},{8,7},{9,10},{10,9},{11,... | collective-permute-start | bytes 147464 | tf_op jit(solution)/shard_map/ppermute | solution.py:48
  10.1 31.5 %collective-permute-start.4 = (bf16[360,1024]{1,0:T(8,128)(2,1)}, bf16[360,1024]{1,0:T(8,128)(2,1)}, u32[]{:S(2)}, u32[]{:S(2)}) collective-permute-start(bf16[360,1024]{1,0:T(8,128)(2,1)} %atmos_ref.1), channel_id=1, source_target_pairs={{1,2},{2,1},{3,4},{4,3},{5,6},{6,5},{7,8},{8,7},{9,10},{10,9},{11,... | collective-permute-start | bytes 2211848 | tf_op jit(solution)/shard_map/ppermute | solution.py:48
  12.2 6.5 %copy-start.6 = (bf16[32,384]{1,0:T(8,128)(2,1)}, bf16[32,384]{1,0:T(8,128)(2,1)S(1)}, u32[]{:S(2)}) copy-start(bf16[32,384]{1,0:T(8,128)(2,1)S(1)} %get-tuple-element.23.m2.m0.message_ref.p2) | copy-start | bytes 73732
  12.2 7.9 %copy-start.12 = (bf16[76,4,1440]{2,1,0:T(4,128)(2,1)S(1)}, bf16[76,4,1440]{2,1,0:T(4,128)(2,1)}, u32[]{:S(2)}) copy-start(bf16[76,4,1440]{2,1,0:T(4,128)(2,1)} %ocean_ref.3) | copy-start | bytes 2626564
  12.2 7.9 %copy-start.16 = (s32[4,1440]{1,0:T(4,128)S(1)}, s32[4,1440]{1,0:T(4,128)}, u32[]{:S(2)}) copy-start(s32[4,1440]{1,0:T(4,128)} %mask_ref.1) | copy-start | bytes 69124
  18.6 6.0 %copy-start = (bf16[360,1024]{1,0:T(8,128)(2,1)}, bf16[360,1024]{1,0:T(8,128)(2,1)S(1)}, u32[]{:S(2)}) copy-start(bf16[360,1024]{1,0:T(8,128)(2,1)S(1)} %get-tuple-element.12.after_ref.q_ref) | copy-start | bytes 2211844
  18.6 6.0 %collective-permute-start.5 = (bf16[360,2048]{1,0:T(8,128)(2,1)}, bf16[360,2048]{1,0:T(8,128)(2,1)}, u32[]{:S(2)}, u32[]{:S(2)}) collective-permute-start(bf16[360,2048]{1,0:T(8,128)(2,1)} %get-tuple-element.13.kv0), channel_id=1, source_target_pairs={{0,1},{1,0},{2,3},{3,2},{4,5},{5,4},{6,7},{7,6},{8,9},{9,8},{10,11... | collective-permute-start | bytes 4423688 | tf_op jit(solution)/shard_map/ppermute | solution.py:40
  21.7 19.9 %copy-start.9 = (bf16[1024,3072]{1,0:T(8,128)(2,1)S(1)}, bf16[1024,3072]{1,0:T(8,128)(2,1)}, u32[]{:S(2)}) copy-start(bf16[1024,3072]{1,0:T(8,128)(2,1)} %w_ref.3) | copy-start | bytes 18874372
  21.7 19.9 %copy-start.7 = (bf16[32,384]{1,0:T(8,128)(2,1)S(1)}, bf16[32,384]{1,0:T(8,128)(2,1)}, u32[]{:S(2)}) copy-start(bf16[32,384]{1,0:T(8,128)(2,1)} %copy-done.6) | copy-start | bytes 73732
  21.7 38.8 %collective-permute-start.2 = (bf16[4,80,1536]{2,1,0:T(8,128)(2,1)}, bf16[4,80,1536]{2,1,0:T(8,128)(2,1)}, u32[]{:S(2)}, u32[]{:S(2)}) collective-permute-start(bf16[4,80,1536]{2,1,0:T(8,128)(2,1)} %gate.1.x0), channel_id=1, source_target_pairs={{0,1},{1,0},{2,3},{3,2},{4,5},{5,4},{6,7},{7,6},{8,9},{9,8},{10,11... | collective-permute-start | bytes 2949128 | tf_op jit(solution)/shard_map/ppermute | solution.py:40
  21.8 38.8 %collective-permute-start.3 = (bf16[4,80,1536]{2,1,0:T(8,128)(2,1)}, bf16[4,80,1536]{2,1,0:T(8,128)(2,1)}, u32[]{:S(2)}, u32[]{:S(2)}) collective-permute-start(bf16[4,80,1536]{2,1,0:T(8,128)(2,1)} %gate.1.x0), channel_id=1, source_target_pairs={{1,2},{2,1},{3,4},{4,3},{5,6},{6,5},{7,8},{8,7},{9,10},{10,9},{11,... | collective-permute-start | bytes 2949128 | tf_op jit(solution)/shard_map/ppermute | solution.py:48
  41.6 4.1 %copy-start.1 = (bf16[360,1024]{1,0:T(8,128)(2,1)S(1)}, bf16[360,1024]{1,0:T(8,128)(2,1)}, u32[]{:S(2)}) copy-start(bf16[360,1024]{1,0:T(8,128)(2,1)} %copy-done) | copy-start | bytes 2211844
  41.6 4.1 %copy-start.10 = (bf16[1024,1024]{1,0:T(8,128)(2,1)S(1)}, bf16[1024,1024]{1,0:T(8,128)(2,1)}, u32[]{:S(2)}) copy-start(bf16[1024,1024]{1,0:T(8,128)(2,1)} %wo_ref.1) | copy-start | bytes 6291460
  41.6 4.1 %copy-start.15 = (bf16[1024,16]{0,1:T(8,128)(2,1)S(1)}, bf16[1024,16]{0,1:T(8,128)(2,1)}, u32[]{:S(2)}) copy-start(bf16[1024,16]{0,1:T(8,128)(2,1)} %param.24) | copy-start | bytes 98308
  41.7 4.1 %copy-start.19 = (f32[1024]{0:T(1024)S(1)}, f32[1024]{0:T(1024)}, u32[]{:S(2)}) copy-start(f32[1024]{0:T(1024)} %param.23) | copy-start | bytes 12292
  45.7 15.6 %copy-start.3 = (bf16[32,384]{1,0:T(8,128)(2,1)S(1)}, bf16[32,384]{1,0:T(8,128)(2,1)}, u32[]{:S(2)}) copy-start(bf16[32,384]{1,0:T(8,128)(2,1)} %copy-done.2) | copy-start | bytes 73732
  45.7 15.6 %copy-start.5 = (bf16[32,384]{1,0:T(8,128)(2,1)S(1)}, bf16[32,384]{1,0:T(8,128)(2,1)}, u32[]{:S(2)}) copy-start(bf16[32,384]{1,0:T(8,128)(2,1)} %copy-done.4) | copy-start | bytes 73732
  45.8 15.6 %copy-start.13 = (bf16[9,128,92]{1,2,0:T(8,128)(2,1)S(1)}, bf16[9,128,92]{1,2,0:T(8,128)(2,1)}, u32[]{:S(2)}) copy-start(bf16[9,128,92]{1,2,0:T(8,128)(2,1)} %param.30) | copy-start | bytes 635908
  45.8 15.6 %copy-start.14 = (bf16[9,76,128]{2,1,0:T(8,128)(2,1)S(1)}, bf16[9,76,128]{2,1,0:T(8,128)(2,1)}, u32[]{:S(2)}) copy-start(bf16[9,76,128]{2,1,0:T(8,128)(2,1)} %c2_ref.1) | copy-start | bytes 525316
  53.1 1.2 %collective-permute-start.6 = (bf16[16,384]{1,0:T(8,128)(2,1)S(1)}, bf16[16,384]{1,0:T(8,128)(2,1)S(1)}, u32[]{:S(2)}, u32[]{:S(2)}) collective-permute-start(bf16[16,384]{1,0:T(8,128)(2,1)S(1)} %get-tuple-element.18.f0), channel_id=1, source_target_pairs={{0,1},{1,0},{2,3},{3,2},{4,5},{5,4},{6,7},{7,6},{8,9},{9,8},{10,11... | collective-permute-start | bytes 36872 | tf_op jit(solution)/shard_map/ppermute | solution.py:40
  54.3 5.4 %collective-permute-start.7 = (bf16[2,16,384]{2,1,0:T(8,128)(2,1)S(1)}, bf16[2,16,384]{2,1,0:T(8,128)(2,1)S(1)}, u32[]{:S(2)}, u32[]{:S(2)}) collective-permute-start(bf16[2,16,384]{2,1,0:T(8,128)(2,1)S(1)} %pad_maximum_fusion.1), channel_id=1, source_target_pairs={{1,2},{2,1},{3,4},{4,3},{5,6},{6,5},{7,8},{8,7},{9,10},{10,9},{11,... | collective-permute-start | bytes 73736 | tf_op jit(solution)/shard_map/ppermute | solution.py:48
  59.7 1.6 %collective-permute-start.8 = (bf16[2,16,384]{2,1,0:T(8,128)(2,1)S(1)}, bf16[2,16,384]{2,1,0:T(8,128)(2,1)S(1)}, u32[]{:S(2)}, u32[]{:S(2)}) collective-permute-start(bf16[2,16,384]{2,1,0:T(8,128)(2,1)S(1)} %collective-permute-done.7.fx), channel_id=1, source_target_pairs={{0,1},{1,0},{2,3},{3,2},{4,5},{5,4},{6,7},{7,6},{8,9},{9,8},{10,11... | collective-permute-start | bytes 73736 | tf_op jit(solution)/shard_map/ppermute | solution.py:40
where the time goes:
time: 83.2 us; the launch traced here: 82.9 us
  Pallas kernels  52.9 us (64%)
  starting transfers between devices  13.5 us (16%)
  waiting for transfers between devices  11.2 us (13%)
  local copies, waits for them, and re-layouts  2.05 us (2%)
  between operations  1.74 us (2%)
  other arithmetic  1.41 us (2%)
    pallas_call x1, Pallas kernels, ocean(): pl.pallas_call(functools.partial(ocean_kernel, channels, count), out_shap...  21.3 us
    pallas_call x1, Pallas kernels, attend_near(): pl.pallas_call(functools.partial(near_kernel, head_count), out_shape=(sha...  11.9 us
    ppermute x4, starting transfers between devices, swap_across(): return lax.ppermute(block, 'lat', pairs)  10.5 us
    pallas_call x2, Pallas kernels, project(): pl.pallas_call(functools.partial(project_kernel, with_query, orows), out_...  10.4 us
    ppermute x4, waiting for transfers between devices, swap_across(): return lax.ppermute(block, 'lat', pairs)  8.35 us
    pallas_call x1, Pallas kernels, attend_far(): pl.pallas_call(functools.partial(far_kernel, head_count), out_shape=(jax....  7.33 us
    ppermute x5, starting transfers between devices, swap_in_chip(): return lax.ppermute(block, 'lat', [(i, i ^ 1) for i in range(count)])  2.98 us
    ppermute x5, waiting for transfers between devices, swap_in_chip(): return lax.ppermute(block, 'lat', [(i, i ^ 1) for i in range(count)])  2.89 us
  transfers between devices with their start and end apart: 9, of which 5 were waited for; matrix products, arithmetic and copies ran while one was open for 0% of the time, Pallas kernels for 38%

commit v1 on v0

--- a/solution.py
+++ b/solution.py
@@ -98,14 +98,16 @@
 def surface_message(pos, ocean_state, surf_start, surf_weight, flux_start, flux_weight):
     channels, orows, olon = ocean_state.shape
     width = up_to(olon // SPAN, LANE)
-    small = jnp.concatenate(
-        [
-            surf_weight.reshape(-1),
-            flux_weight.T.reshape(-1),
-            flux_start.astype(F32),
-            surf_start.astype(F32),
-        ]
-    ).reshape(1, -1)
+    bands = flux_weight.T
+    pieces = [surf_weight, bands[0:1], bands[1:2]]
+    pieces += [flux_start.astype(F32).reshape(1, -1), surf_start.astype(F32).reshape(1, -1)]
+    lanes = sum(piece.shape[1] for piece in pieces)
+    small, at = None, 0
+    for piece in pieces:
+        size = piece.shape[1]
+        padded = jnp.pad(piece, ((0, 0), (at, lanes - at - size)))
+        small = padded if small is None else small + padded
+        at += size
     return pl.pallas_call(
         surface_kernel,
         out_shape=jax.ShapeDtypeStruct((32, width), BF16),
@@ -417,9 +419,10 @@
     w1_ref[...] = w1t[...].T.astype(BF16)
 
     def put_state(row, values):
-        zbuf[row, 0:deep] = pltpu.roll(values, 1, 1).astype(BF16)
-        zbuf[row, deep : 2 * deep] = values.astype(BF16)
-        zbuf[row, 2 * deep : 3 * deep] = pltpu.roll(values, width - 1, 1).astype(BF16)
+        values = values.astype(BF16)
+        zbuf[row, 0:deep] = pltpu.roll(values, 1, 1)
+        zbuf[row, deep : 2 * deep] = values
+        zbuf[row, 2 * deep : 3 * deep] = pltpu.roll(values, width - 1, 1)
 
     blocks = (
         (x0, p0, orows),
@@ -475,9 +478,10 @@
         place = position * orows + row
         keep = (place >= 0) & (place < count * orows)
         values = values * jnp.where(keep, 1.0, 0.0).astype(F32)
-        hbuf[slot, 0:hid] = pltpu.roll(values, 1, 1).astype(BF16)
-        hbuf[slot, hid : 2 * hid] = values.astype(BF16)
-        hbuf[slot, 2 * hid : 3 * hid] = pltpu.roll(values, width - 1, 1).astype(BF16)
+        values = values.astype(BF16)
+        hbuf[slot, 0:hid] = pltpu.roll(values, 1, 1)
+        hbuf[slot, hid : 2 * hid] = values
+        hbuf[slot, 2 * hid : 3 * hid] = pltpu.roll(values, width - 1, 1)
 
     def pair_update(hrow, srow):
         taps = hbuf[pl.ds(hrow, 4)].reshape(4 * 3 * hid, width)

time: 83.2 us -> 79.9 us (0.960)
  Pallas kernels: 52.9 us -> 49.6 us
    pallas_call x1, Pallas kernels: 21.3 us -> 18 us  [ocean(): pl.pallas_call(functools.partial(ocean_kernel, channels, count), out_shap...]
  transfers between devices with their start and end apart: 9 -> 9, of which waited for: 5 -> 5; matrix products, arithmetic and copies ran while one was open for 0% -> 0% of each run, Pallas kernels for 38% -> 39%
where the time goes in v1:
time: 79.9 us; the launch traced here: 79.6 us
  Pallas kernels  49.6 us (62%)
  starting transfers between devices  13.5 us (17%)
  waiting for transfers between devices  11.2 us (14%)
  local copies, waits for them, and re-layouts  2.05 us (3%)
  between operations  1.75 us (2%)
  other arithmetic  1.41 us (2%)
    pallas_call x1, Pallas kernels, ocean(): pl.pallas_call(functools.partial(ocean_kernel, channels, count), out_shap...  18 us
    pallas_call x1, Pallas kernels, attend_near(): pl.pallas_call(functools.partial(near_kernel, head_count), out_shape=(sha...  11.9 us
    ppermute x4, starting transfers between devices, swap_across(): return lax.ppermute(block, 'lat', pairs)  10.5 us
    pallas_call x2, Pallas kernels, project(): pl.pallas_call(functools.partial(project_kernel, with_query, orows), out_...  10.4 us
    ppermute x4, waiting for transfers between devices, swap_across(): return lax.ppermute(block, 'lat', pairs)  8.34 us
    pallas_call x1, Pallas kernels, attend_far(): pl.pallas_call(functools.partial(far_kernel, head_count), out_shape=(jax....  7.33 us
    ppermute x5, starting transfers between devices, swap_in_chip(): return lax.ppermute(block, 'lat', [(i, i ^ 1) for i in range(count)])  2.98 us
    ppermute x5, waiting for transfers between devices, swap_in_chip(): return lax.ppermute(block, 'lat', [(i, i ^ 1) for i in range(count)])  2.89 us
  transfers between devices with their start and end apart: 9, of which 5 were waited for; matrix products, arithmetic and copies ran while one was open for 0% of the time, Pallas kernels for 39%

profile of v1, /device:TPU:25, one launch (start us, length us, event | category | flops | bytes accessed | tf_op | source)
XLA Modules:
  0.0 79.6 jit_solution(15700464368239004510)
XLA Ops:
  0.6 0.8 fusion
  2.0 0.7 convert_bitcast_fusion
  2.7 0.7 pad_add_fusion.small_ref
  3.4 1.2 %copy-done.11 = bf16[76,4,1440]{2,1,0:T(4,128)(2,1)S(1)} copy-done((bf16[76,4,1440]{2,1,0:T(4,128)(2,1)S(1)}, bf16[76,4,1440]{2,1,0:T(4,128)(2,1)}, u32[]{:S(2)}) %copy-start.11) | copy-done | bytes 875544
  4.6 0.3 surface.1.m0.after_ref.m1.p0
  4.9 0.0 copy-start.2
  5.0 0.7 collective-permute-start
  5.7 0.8 %collective-permute-done.m1.p1 = bf16[32,384]{1,0:T(8,128)(2,1)S(1)} collective-permute-done((bf16[32,384]{1,0:T(8,128)(2,1)S(1)}, bf16[32,384]{1,0:T(8,128)(2,1)S(1)}, u32[]{:S(2)}, u32[]{:S(2)}) %collective-permute-start) | collective-permute-done | bytes 24608 | tf_op jit(solution)/shard_map/ppermute | solution.py:40
  6.6 3.5 %collective-permute-start.1 = (bf16[2,32,384]{2,1,0:T(8,128)(2,1)S(1)}, bf16[2,32,384]{2,1,0:T(8,128)(2,1)S(1)}, u32[]{:S(2)}, u32[]{:S(2)}) collective-permute-start(bf16[2,32,384]{2,1,0:T(8,128)(2,1)S(1)} %pad_maximum_fusion), channel_id=1, source_target_pairs={{1,2},{2,1},{3,4},{4,3},{5,6},{6,5},{7,8},{8,7},{9,10},{10,9},{11,... | collective-permute-start | bytes 147464 | tf_op jit(solution)/shard_map/ppermute | solution.py:48
  10.1 2.1 %collective-permute-start.4 = (bf16[360,1024]{1,0:T(8,128)(2,1)}, bf16[360,1024]{1,0:T(8,128)(2,1)}, u32[]{:S(2)}, u32[]{:S(2)}) collective-permute-start(bf16[360,1024]{1,0:T(8,128)(2,1)} %atmos_ref.1), channel_id=1, source_target_pairs={{1,2},{2,1},{3,4},{4,3},{5,6},{6,5},{7,8},{8,7},{9,10},{10,9},{11,... | collective-permute-start | bytes 2211848 | tf_op jit(solution)/shard_map/ppermute | solution.py:48
  12.2 0.0 copy-start.12
  12.2 0.0 copy-start.16
  12.2 6.4 %project.2 = (f32[360,1024]{1,0:T(8,128)S(1)}, bf16[360,1024]{1,0:T(8,128)(2,1)S(1)}, bf16[360,2048]{1,0:T(8,128)(2,1)}) custom-call(s32[1]{0:T(128)} %bitcast.pos_ref, f32[16]{0:T(128)S(1)} %copy-done.20, bf16[360,1024]{1,0:T(8,128)(2,1)} %atmos_ref.1, bf16[32,384]{1,0:T(8,128)(2,1)S(1)} %surface.1.m0.after_ref.m1.p0, ...), custom_call_target="tpu_custom_call" | custom-call | flops 999999995904 | bytes 1000000000 | tf_op jit(solution)/shard_map/project/pallas_call | solution.py:243
  18.7 1.4 %collective-permute-start.5 = (bf16[360,2048]{1,0:T(8,128)(2,1)}, bf16[360,2048]{1,0:T(8,128)(2,1)}, u32[]{:S(2)}, u32[]{:S(2)}) collective-permute-start(bf16[360,2048]{1,0:T(8,128)(2,1)} %get-tuple-element.13.kv0), channel_id=1, source_target_pairs={{0,1},{1,0},{2,3},{3,2},{4,5},{5,4},{6,7},{7,6},{8,9},{9,8},{10,11... | collective-permute-start | bytes 4423688 | tf_op jit(solution)/shard_map/ppermute | solution.py:40
  20.1 1.6 %relayout.1.value_ref = bf16[4,80,1536]{2,1,0:T(8,128)(2,1)} custom-call(bf16[76,4,1440]{2,1,0:T(4,128)(2,1)S(1)} %copy-done.12, s32[4,1440]{1,0:T(4,128)S(1)} %copy-done.16, bf16[360,1024]{1,0:T(8,128)(2,1)S(1)} %get-tuple-element.12.after_ref.q_ref), custom_call_target="tpu_custom_call" | custom-call | flops 999999995904 | bytes 1000000000 | tf_op jit(solution)/shard_map/relayout/pallas_call | solution.py:149
  21.7 0.0 collective-permute-start.2
  21.8 2.9 %collective-permute-start.3 = (bf16[4,80,1536]{2,1,0:T(8,128)(2,1)}, bf16[4,80,1536]{2,1,0:T(8,128)(2,1)}, u32[]{:S(2)}, u32[]{:S(2)}) collective-permute-start(bf16[4,80,1536]{2,1,0:T(8,128)(2,1)} %gate.1.x0), channel_id=1, source_target_pairs={{1,2},{2,1},{3,4},{4,3},{5,6},{6,5},{7,8},{8,7},{9,10},{10,9},{11,... | collective-permute-start | bytes 2949128 | tf_op jit(solution)/shard_map/ppermute | solution.py:48
  24.7 11.9 %near.1 = (f32[360,1024]{1,0:T(8,128)S(1)}, f32[360,1024]{1,0:T(8,128)S(1)}, f32[360,1024]{1,0:T(8,128)S(1)}) custom-call(bf16[360,1024]{1,0:T(8,128)(2,1)S(1)} %get-tuple-element.12.after_ref.q_ref, bf16[360,2048]{1,0:T(8,128)(2,1)} %get-tuple-element.13.kv0, bf16[360,2048]{1,0:T(8,128)(2,1)} %collective-permute-done.5.kv1), custom_call_target="tpu_custom_call" | custom-call | flops 1 | bytes 1 | tf_op jit(solution)/shard_map/near/pallas_call | solution.py:301
  36.6 5.0 %collective-permute-done.4.atmos_ref = bf16[360,1024]{1,0:T(8,128)(2,1)} collective-permute-done((bf16[360,1024]{1,0:T(8,128)(2,1)}, bf16[360,1024]{1,0:T(8,128)(2,1)}, u32[]{:S(2)}, u32[]{:S(2)}) %collective-permute-start.4) | collective-permute-done | bytes 737312 | tf_op jit(solution)/shard_map/ppermute | solution.py:48
  41.6 0.0 copy-start.1
  41.6 0.0 copy-start.10
  41.7 0.0 copy-start.19
  41.7 4.0 %project.3.kv_ref = bf16[360,2048]{1,0:T(8,128)(2,1)S(1)} custom-call(s32[1]{0:T(128)} %bitcast.pos_ref, f32[16]{0:T(128)S(1)} %copy-done.20, bf16[360,1024]{1,0:T(8,128)(2,1)} %collective-permute-done.4.atmos_ref, bf16[32,384]{1,0:T(8,128)(2,1)S(1)} %copy-done.7, bf16[32,384]{1,0:T(8,128)(2,1)S(1)} %surface.1.m0.after_ref.m1.p0, ...), custom_call_target="tpu_custom_call" | custom-call | flops 999999995904 | bytes 1000000000 | tf_op jit(solution)/shard_map/project/pallas_call | solution.py:243
  45.7 0.0 copy-start.3
  45.8 0.0 copy-start.13
  45.8 7.3 %far.1 = (bf16[360,1024]{1,0:T(8,128)(2,1)S(1)}, bf16[16,384]{1,0:T(8,128)(2,1)S(1)}) custom-call(bf16[32,384]{1,0:T(8,128)(2,1)S(1)} %copy-done.7, bf16[360,1024]{1,0:T(8,128)(2,1)S(1)} %copy-done.1, bf16[360,2048]{1,0:T(8,128)(2,1)S(1)} %project.3.kv_ref, f32[360,1024]{1,0:T(8,128)S(1)} %get-tuple-element.14.after_ref.top_ref, ...), custom_call_target="tpu_custom_call" | custom-call | flops 999999995904 | bytes 1000000000 | tf_op jit(solution)/shard_map/far/pallas_call | solution.py:349
  53.1 1.2 %collective-permute-done.6.f1 = bf16[16,384]{1,0:T(8,128)(2,1)S(1)} collective-permute-done((bf16[16,384]{1,0:T(8,128)(2,1)S(1)}, bf16[16,384]{1,0:T(8,128)(2,1)S(1)}, u32[]{:S(2)}, u32[]{:S(2)}) %collective-permute-start.6) | collective-permute-done | bytes 12320 | tf_op jit(solution)/shard_map/ppermute | solution.py:40
  54.3 2.1 %collective-permute-start.7 = (bf16[2,16,384]{2,1,0:T(8,128)(2,1)S(1)}, bf16[2,16,384]{2,1,0:T(8,128)(2,1)S(1)}, u32[]{:S(2)}, u32[]{:S(2)}) collective-permute-start(bf16[2,16,384]{2,1,0:T(8,128)(2,1)S(1)} %pad_maximum_fusion.1), channel_id=1, source_target_pairs={{1,2},{2,1},{3,4},{4,3},{5,6},{6,5},{7,8},{8,7},{9,10},{10,9},{11,... | collective-permute-start | bytes 73736 | tf_op jit(solution)/shard_map/ppermute | solution.py:48
  56.4 3.3 %collective-permute-done.7.fx = bf16[2,16,384]{2,1,0:T(8,128)(2,1)S(1)} collective-permute-done((bf16[2,16,384]{2,1,0:T(8,128)(2,1)S(1)}, bf16[2,16,384]{2,1,0:T(8,128)(2,1)S(1)}, u32[]{:S(2)}, u32[]{:S(2)}) %collective-permute-start.7) | collective-permute-done | bytes 24608 | tf_op jit(solution)/shard_map/ppermute | solution.py:48
  59.8 0.8 collective-permute-start.8
  60.5 0.8 %collective-permute-done.8.fy = bf16[2,16,384]{2,1,0:T(8,128)(2,1)S(1)} collective-permute-done((bf16[2,16,384]{2,1,0:T(8,128)(2,1)S(1)}, bf16[2,16,384]{2,1,0:T(8,128)(2,1)S(1)}, u32[]{:S(2)}, u32[]{:S(2)}) %collective-permute-start.8) | collective-permute-done | bytes 24608 | tf_op jit(solution)/shard_map/ppermute | solution.py:40
  61.4 18.0 %ocean.1 = (bf16[76,4,1440]{2,1,0:T(4,128)(2,1)}, bf16[360,1024]{1,0:T(8,128)(2,1)}) custom-call(s32[1]{0:T(128)} %bitcast.pos_ref, bf16[4,80,1536]{2,1,0:T(8,128)(2,1)} %gate.1.x0, bf16[4,80,1536]{2,1,0:T(8,128)(2,1)} %collective-permute-done.2.x1, bf16[4,80,1536]{2,1,0:T(8,128)(2,1)} %collective-permute-done.3.x2, bf16[32,384]{1,0:T(8,128)(2,1)S(1)} %copy-done.3, ...), custom_call_target="tpu_custom_call" | custom-call | flops 20000000000 | bytes 10000000 | tf_op jit(solution)/shard_map/ocean/pallas_call | solution.py:526
  (42 shorter events, 0.1 us)
Async XLA Ops:
  3.4 1.2 %copy-start.11 = (bf16[76,4,1440]{2,1,0:T(4,128)(2,1)S(1)}, bf16[76,4,1440]{2,1,0:T(4,128)(2,1)}, u32[]{:S(2)}) copy-start(bf16[76,4,1440]{2,1,0:T(4,128)(2,1)} %ocean_ref.3) | copy-start | bytes 2626564
  4.6 7.6 %copy-start.8 = (bf16[1024,3072]{1,0:T(8,128)(2,1)S(1)}, bf16[1024,3072]{1,0:T(8,128)(2,1)}, u32[]{:S(2)}) copy-start(bf16[1024,3072]{1,0:T(8,128)(2,1)} %w_ref.3) | copy-start | bytes 18874372
  4.6 7.6 %copy-start.17 = (f32[4,1024]{1,0:T(4,128)S(1)}, f32[4,1024]{1,0:T(4,128)}, u32[]{:S(2)}) copy-start(f32[4,1024]{1,0:T(4,128)} %embed_ref.3) | copy-start | bytes 49156
  4.6 7.6 %copy-start.18 = (f32[1024]{0:T(1024)S(1)}, f32[1024]{0:T(1024)}, u32[]{:S(2)}) copy-start(f32[1024]{0:T(1024)} %param.22) | copy-start | bytes 12292
  4.6 7.6 %copy-start.20 = (f32[16]{0:T(128)S(1)}, f32[16]{0:T(128)}, u32[]{:S(2)}) copy-start(f32[16]{0:T(128)} %scale_ref.3) | copy-start | bytes 196
  4.9 36.7 %copy-start.2 = (bf16[32,384]{1,0:T(8,128)(2,1)}, bf16[32,384]{1,0:T(8,128)(2,1)S(1)}, u32[]{:S(2)}) copy-start(bf16[32,384]{1,0:T(8,128)(2,1)S(1)} %surface.1.m0.after_ref.m1.p0) | copy-start | bytes 73732
  5.0 1.6 %collective-permute-start = (bf16[32,384]{1,0:T(8,128)(2,1)S(1)}, bf16[32,384]{1,0:T(8,128)(2,1)S(1)}, u32[]{:S(2)}, u32[]{:S(2)}) collective-permute-start(bf16[32,384]{1,0:T(8,128)(2,1)S(1)} %surface.1.m0.after_ref.m1.p0), channel_id=1, source_target_pairs={{0,1},{1,0},{2,3},{3,2},{4,5},{5,4},{6,7},{7,6},{8,9},{9,8},{10,11... | collective-permute-start | bytes 73736 | tf_op jit(solution)/shard_map/ppermute | solution.py:40
  6.5 12.1 %copy-start.4 = (bf16[32,384]{1,0:T(8,128)(2,1)}, bf16[32,384]{1,0:T(8,128)(2,1)S(1)}, u32[]{:S(2)}) copy-start(bf16[32,384]{1,0:T(8,128)(2,1)S(1)} %collective-permute-done.m1.p1) | copy-start | bytes 73732
  6.6 5.6 %collective-permute-start.1 = (bf16[2,32,384]{2,1,0:T(8,128)(2,1)S(1)}, bf16[2,32,384]{2,1,0:T(8,128)(2,1)S(1)}, u32[]{:S(2)}, u32[]{:S(2)}) collective-permute-start(bf16[2,32,384]{2,1,0:T(8,128)(2,1)S(1)} %pad_maximum_fusion), channel_id=1, source_target_pairs={{1,2},{2,1},{3,4},{4,3},{5,6},{6,5},{7,8},{8,7},{9,10},{10,9},{11,... | collective-permute-start | bytes 147464 | tf_op jit(solution)/shard_map/ppermute | solution.py:48
  10.1 31.5 %collective-permute-start.4 = (bf16[360,1024]{1,0:T(8,128)(2,1)}, bf16[360,1024]{1,0:T(8,128)(2,1)}, u32[]{:S(2)}, u32[]{:S(2)}) collective-permute-start(bf16[360,1024]{1,0:T(8,128)(2,1)} %atmos_ref.1), channel_id=1, source_target_pairs={{1,2},{2,1},{3,4},{4,3},{5,6},{6,5},{7,8},{8,7},{9,10},{10,9},{11,... | collective-permute-start | bytes 2211848 | tf_op jit(solution)/shard_map/ppermute | solution.py:48
  12.2 6.5 %copy-start.6 = (bf16[32,384]{1,0:T(8,128)(2,1)}, bf16[32,384]{1,0:T(8,128)(2,1)S(1)}, u32[]{:S(2)}) copy-start(bf16[32,384]{1,0:T(8,128)(2,1)S(1)} %get-tuple-element.23.m2.m0.message_ref.p2) | copy-start | bytes 73732
  12.2 7.9 %copy-start.12 = (bf16[76,4,1440]{2,1,0:T(4,128)(2,1)S(1)}, bf16[76,4,1440]{2,1,0:T(4,128)(2,1)}, u32[]{:S(2)}) copy-start(bf16[76,4,1440]{2,1,0:T(4,128)(2,1)} %ocean_ref.3) | copy-start | bytes 2626564
  12.2 7.9 %copy-start.16 = (s32[4,1440]{1,0:T(4,128)S(1)}, s32[4,1440]{1,0:T(4,128)}, u32[]{:S(2)}) copy-start(s32[4,1440]{1,0:T(4,128)} %mask_ref.1) | copy-start | bytes 69124
  18.7 6.0 %copy-start = (bf16[360,1024]{1,0:T(8,128)(2,1)}, bf16[360,1024]{1,0:T(8,128)(2,1)S(1)}, u32[]{:S(2)}) copy-start(bf16[360,1024]{1,0:T(8,128)(2,1)S(1)} %get-tuple-element.12.after_ref.q_ref) | copy-start | bytes 2211844
  18.7 6.0 %collective-permute-start.5 = (bf16[360,2048]{1,0:T(8,128)(2,1)}, bf16[360,2048]{1,0:T(8,128)(2,1)}, u32[]{:S(2)}, u32[]{:S(2)}) collective-permute-start(bf16[360,2048]{1,0:T(8,128)(2,1)} %get-tuple-element.13.kv0), channel_id=1, source_target_pairs={{0,1},{1,0},{2,3},{3,2},{4,5},{5,4},{6,7},{7,6},{8,9},{9,8},{10,11... | collective-permute-start | bytes 4423688 | tf_op jit(solution)/shard_map/ppermute | solution.py:40
  21.7 19.9 %copy-start.9 = (bf16[1024,3072]{1,0:T(8,128)(2,1)S(1)}, bf16[1024,3072]{1,0:T(8,128)(2,1)}, u32[]{:S(2)}) copy-start(bf16[1024,3072]{1,0:T(8,128)(2,1)} %w_ref.3) | copy-start | bytes 18874372
  21.7 19.9 %copy-start.7 = (bf16[32,384]{1,0:T(8,128)(2,1)S(1)}, bf16[32,384]{1,0:T(8,128)(2,1)}, u32[]{:S(2)}) copy-start(bf16[32,384]{1,0:T(8,128)(2,1)} %copy-done.6) | copy-start | bytes 73732
  21.7 38.8 %collective-permute-start.2 = (bf16[4,80,1536]{2,1,0:T(8,128)(2,1)}, bf16[4,80,1536]{2,1,0:T(8,128)(2,1)}, u32[]{:S(2)}, u32[]{:S(2)}) collective-permute-start(bf16[4,80,1536]{2,1,0:T(8,128)(2,1)} %gate.1.x0), channel_id=1, source_target_pairs={{0,1},{1,0},{2,3},{3,2},{4,5},{5,4},{6,7},{7,6},{8,9},{9,8},{10,11... | collective-permute-start | bytes 2949128 | tf_op jit(solution)/shard_map/ppermute | solution.py:40
  21.8 38.7 %collective-permute-start.3 = (bf16[4,80,1536]{2,1,0:T(8,128)(2,1)}, bf16[4,80,1536]{2,1,0:T(8,128)(2,1)}, u32[]{:S(2)}, u32[]{:S(2)}) collective-permute-start(bf16[4,80,1536]{2,1,0:T(8,128)(2,1)} %gate.1.x0), channel_id=1, source_target_pairs={{1,2},{2,1},{3,4},{4,3},{5,6},{6,5},{7,8},{8,7},{9,10},{10,9},{11,... | collective-permute-start | bytes 2949128 | tf_op jit(solution)/shard_map/ppermute | solution.py:48
  41.6 4.1 %copy-start.1 = (bf16[360,1024]{1,0:T(8,128)(2,1)S(1)}, bf16[360,1024]{1,0:T(8,128)(2,1)}, u32[]{:S(2)}) copy-start(bf16[360,1024]{1,0:T(8,128)(2,1)} %copy-done) | copy-start | bytes 2211844
  41.6 4.1 %copy-start.10 = (bf16[1024,1024]{1,0:T(8,128)(2,1)S(1)}, bf16[1024,1024]{1,0:T(8,128)(2,1)}, u32[]{:S(2)}) copy-start(bf16[1024,1024]{1,0:T(8,128)(2,1)} %wo_ref.1) | copy-start | bytes 6291460
  41.7 4.1 %copy-start.15 = (bf16[1024,16]{0,1:T(8,128)(2,1)S(1)}, bf16[1024,16]{0,1:T(8,128)(2,1)}, u32[]{:S(2)}) copy-start(bf16[1024,16]{0,1:T(8,128)(2,1)} %param.24) | copy-start | bytes 98308
  41.7 4.1 %copy-start.19 = (f32[1024]{0:T(1024)S(1)}, f32[1024]{0:T(1024)}, u32[]{:S(2)}) copy-start(f32[1024]{0:T(1024)} %param.23) | copy-start | bytes 12292
  45.7 15.6 %copy-start.3 = (bf16[32,384]{1,0:T(8,128)(2,1)S(1)}, bf16[32,384]{1,0:T(8,128)(2,1)}, u32[]{:S(2)}) copy-start(bf16[32,384]{1,0:T(8,128)(2,1)} %copy-done.2) | copy-start | bytes 73732
  45.8 15.6 %copy-start.5 = (bf16[32,384]{1,0:T(8,128)(2,1)S(1)}, bf16[32,384]{1,0:T(8,128)(2,1)}, u32[]{:S(2)}) copy-start(bf16[32,384]{1,0:T(8,128)(2,1)} %copy-done.4) | copy-start | bytes 73732
  45.8 15.6 %copy-start.13 = (bf16[9,128,92]{1,2,0:T(8,128)(2,1)S(1)}, bf16[9,128,92]{1,2,0:T(8,128)(2,1)}, u32[]{:S(2)}) copy-start(bf16[9,128,92]{1,2,0:T(8,128)(2,1)} %param.30) | copy-start | bytes 635908
  45.8 15.6 %copy-start.14 = (bf16[9,76,128]{2,1,0:T(8,128)(2,1)S(1)}, bf16[9,76,128]{2,1,0:T(8,128)(2,1)}, u32[]{:S(2)}) copy-start(bf16[9,76,128]{2,1,0:T(8,128)(2,1)} %c2_ref.1) | copy-start | bytes 525316
  53.1 1.2 %collective-permute-start.6 = (bf16[16,384]{1,0:T(8,128)(2,1)S(1)}, bf16[16,384]{1,0:T(8,128)(2,1)S(1)}, u32[]{:S(2)}, u32[]{:S(2)}) collective-permute-start(bf16[16,384]{1,0:T(8,128)(2,1)S(1)} %get-tuple-element.18.f0), channel_id=1, source_target_pairs={{0,1},{1,0},{2,3},{3,2},{4,5},{5,4},{6,7},{7,6},{8,9},{9,8},{10,11... | collective-permute-start | bytes 36872 | tf_op jit(solution)/shard_map/ppermute | solution.py:40
  54.3 5.4 %collective-permute-start.7 = (bf16[2,16,384]{2,1,0:T(8,128)(2,1)S(1)}, bf16[2,16,384]{2,1,0:T(8,128)(2,1)S(1)}, u32[]{:S(2)}, u32[]{:S(2)}) collective-permute-start(bf16[2,16,384]{2,1,0:T(8,128)(2,1)S(1)} %pad_maximum_fusion.1), channel_id=1, source_target_pairs={{1,2},{2,1},{3,4},{4,3},{5,6},{6,5},{7,8},{8,7},{9,10},{10,9},{11,... | collective-permute-start | bytes 73736 | tf_op jit(solution)/shard_map/ppermute | solution.py:48
  59.8 1.6 %collective-permute-start.8 = (bf16[2,16,384]{2,1,0:T(8,128)(2,1)S(1)}, bf16[2,16,384]{2,1,0:T(8,128)(2,1)S(1)}, u32[]{:S(2)}, u32[]{:S(2)}) collective-permute-start(bf16[2,16,384]{2,1,0:T(8,128)(2,1)S(1)} %collective-permute-done.7.fx), channel_id=1, source_target_pairs={{0,1},{1,0},{2,3},{3,2},{4,5},{5,4},{6,7},{7,6},{8,9},{9,8},{10,11... | collective-permute-start | bytes 73736 | tf_op jit(solution)/shard_map/ppermute | solution.py:40

commit v2 on v1

--- a/solution.py
+++ b/solution.py
@@ -384,7 +384,7 @@
     return 0.5 * x * (1.0 + jnp.tanh(inner))
 
 
-def ocean_kernel(channels, count, pos_ref, x0, x1, x2, p0, p1, p2, f0, f1, fx, fy, c1_ref, c2_ref, next_ref, out_ref, next_hbm, zbuf, hbuf, state, masks, f_ref, w1_ref, w2_ref, w1t, turned, sem):
+def ocean_kernel(channels, count, pos_ref, x0, x1, x2, p0, p1, p2, f0, f1, fx, fy, c1_ref, c2_ref, next_ref, out_ref, next_hbm, zbuf, hbuf, state, masks, f_ref, w1_ref, w2_ref, w1t, turned, ftot, sem):
     copy = pltpu.make_async_copy(next_ref, next_hbm, sem)
     copy.start()
     orows, deep, width = x0.shape
@@ -459,18 +459,22 @@
             behind = pltpu.roll(total, fwidth - tokens, 1)
             total = jnp.where(flane == tokens, ahead, total)
             total = jnp.where(flane == fwidth - 1, behind, total)
-            total = total.astype(BF16)
-            spread = jnp.concatenate(
-                [
-                    jnp.dot(total[:, at : at + LANE], expand, preferred_element_type=F32)
-                    for at in range(0, fwidth, LANE)
-                ],
-                axis=1,
-            )
-            at = 3 * deep
-            zbuf[row, at : at + nflux] = pltpu.roll(spread, 1, 1).astype(BF16)
-            zbuf[row, at + nflux : at + 2 * nflux] = spread.astype(BF16)
-            zbuf[row, at + 2 * nflux : at + 3 * nflux] = pltpu.roll(spread, width - 1, 1).astype(BF16)
+            ftot[row] = total.astype(BF16)
+    every = ftot[...].reshape(3 * orows * nflux, fwidth)
+    spread = jnp.concatenate(
+        [
+            jnp.dot(every[:, at : at + LANE], expand, preferred_element_type=F32)
+            for at in range(0, fwidth, LANE)
+        ],
+        axis=1,
+    ).astype(BF16)
+    left, right = pltpu.roll(spread, 1, 1), pltpu.roll(spread, width - 1, 1)
+    for row in range(3 * orows):
+        mine = slice(row * nflux, (row + 1) * nflux)
+        at = 3 * deep
+        zbuf[row, at : at + nflux] = left[mine]
+        zbuf[row, at + nflux : at + 2 * nflux] = spread[mine]
+        zbuf[row, at + 2 * nflux : at + 3 * nflux] = right[mine]
 
     def hidden_row(row, zrow, slot):
         taps = zbuf[pl.ds(zrow, 3)].reshape(3 * high, width)
@@ -541,6 +545,7 @@
             pltpu.VMEM((160, 12 * hid), BF16),
             pltpu.VMEM((3 * high, hid), F32),
             pltpu.VMEM((channels, orows, olon), F32),
+            pltpu.VMEM((3 * orows, nflux, fwidth), BF16),
             pltpu.SemaphoreType.DMA,
         ],
         compiler_params=limit(44),

time: 79.9 us -> 79.6 us (level)
  transfers between devices with their start and end apart: 9 -> 9, of which waited for: 5 -> 5; matrix products, arithmetic and copies ran while one was open for 0% -> 0% of each run, Pallas kernels for 39% -> 40%
where the time goes in v2:
time: 79.6 us; the launch traced here: 79.2 us
  Pallas kernels  49.3 us (62%)
  starting transfers between devices  13.5 us (17%)
  waiting for transfers between devices  11.2 us (14%)
  local copies, waits for them, and re-layouts  2.05 us (3%)
  between operations  1.75 us (2%)
  other arithmetic  1.41 us (2%)
    pallas_call x1, Pallas kernels, ocean(): pl.pallas_call(functools.partial(ocean_kernel, channels, count), out_shap...  17.7 us
    pallas_call x1, Pallas kernels, attend_near(): pl.pallas_call(functools.partial(near_kernel, head_count), out_shape=(sha...  11.9 us
    ppermute x4, starting transfers between devices, swap_across(): return lax.ppermute(block, 'lat', pairs)  10.5 us
    pallas_call x2, Pallas kernels, project(): pl.pallas_call(functools.partial(project_kernel, with_query, orows), out_...  10.4 us
    ppermute x4, waiting for transfers between devices, swap_across(): return lax.ppermute(block, 'lat', pairs)  8.34 us
    pallas_call x1, Pallas kernels, attend_far(): pl.pallas_call(functools.partial(far_kernel, head_count), out_shape=(jax....  7.33 us
    ppermute x5, starting transfers between devices, swap_in_chip(): return lax.ppermute(block, 'lat', [(i, i ^ 1) for i in range(count)])  2.98 us
    ppermute x5, waiting for transfers between devices, swap_in_chip(): return lax.ppermute(block, 'lat', [(i, i ^ 1) for i in range(count)])  2.89 us
  transfers between devices with their start and end apart: 9, of which 5 were waited for; matrix products, arithmetic and copies ran while one was open for 0% of the time, Pallas kernels for 40%

profile of v2, /device:TPU:25, one launch (start us, length us, event | category | flops | bytes accessed | tf_op | source)
XLA Modules:
  0.0 79.2 jit_solution(17705676092920559849)
XLA Ops:
  0.6 0.8 fusion
  2.0 0.7 convert_bitcast_fusion
  2.7 0.7 pad_add_fusion.small_ref
  3.4 1.2 %copy-done.11 = bf16[76,4,1440]{2,1,0:T(4,128)(2,1)S(1)} copy-done((bf16[76,4,1440]{2,1,0:T(4,128)(2,1)S(1)}, bf16[76,4,1440]{2,1,0:T(4,128)(2,1)}, u32[]{:S(2)}) %copy-start.11) | copy-done | bytes 875544
  4.6 0.3 surface.1.m0.after_ref.m1.p0
  4.9 0.0 copy-start.2
  5.0 0.7 collective-permute-start
  5.7 0.8 %collective-permute-done.m1.p1 = bf16[32,384]{1,0:T(8,128)(2,1)S(1)} collective-permute-done((bf16[32,384]{1,0:T(8,128)(2,1)S(1)}, bf16[32,384]{1,0:T(8,128)(2,1)S(1)}, u32[]{:S(2)}, u32[]{:S(2)}) %collective-permute-start) | collective-permute-done | bytes 24608 | tf_op jit(solution)/shard_map/ppermute | solution.py:40
  6.6 3.5 %collective-permute-start.1 = (bf16[2,32,384]{2,1,0:T(8,128)(2,1)S(1)}, bf16[2,32,384]{2,1,0:T(8,128)(2,1)S(1)}, u32[]{:S(2)}, u32[]{:S(2)}) collective-permute-start(bf16[2,32,384]{2,1,0:T(8,128)(2,1)S(1)} %pad_maximum_fusion), channel_id=1, source_target_pairs={{1,2},{2,1},{3,4},{4,3},{5,6},{6,5},{7,8},{8,7},{9,10},{10,9},{11,... | collective-permute-start | bytes 147464 | tf_op jit(solution)/shard_map/ppermute | solution.py:48
  10.1 2.1 %collective-permute-start.4 = (bf16[360,1024]{1,0:T(8,128)(2,1)}, bf16[360,1024]{1,0:T(8,128)(2,1)}, u32[]{:S(2)}, u32[]{:S(2)}) collective-permute-start(bf16[360,1024]{1,0:T(8,128)(2,1)} %atmos_ref.1), channel_id=1, source_target_pairs={{1,2},{2,1},{3,4},{4,3},{5,6},{6,5},{7,8},{8,7},{9,10},{10,9},{11,... | collective-permute-start | bytes 2211848 | tf_op jit(solution)/shard_map/ppermute | solution.py:48
  12.2 0.0 copy-start.12
  12.2 0.0 copy-start.16
  12.2 6.4 %project.2 = (f32[360,1024]{1,0:T(8,128)S(1)}, bf16[360,1024]{1,0:T(8,128)(2,1)S(1)}, bf16[360,2048]{1,0:T(8,128)(2,1)}) custom-call(s32[1]{0:T(128)} %bitcast.pos_ref, f32[16]{0:T(128)S(1)} %copy-done.20, bf16[360,1024]{1,0:T(8,128)(2,1)} %atmos_ref.1, bf16[32,384]{1,0:T(8,128)(2,1)S(1)} %surface.1.m0.after_ref.m1.p0, ...), custom_call_target="tpu_custom_call" | custom-call | flops 999999995904 | bytes 1000000000 | tf_op jit(solution)/shard_map/project/pallas_call | solution.py:243
  18.7 1.4 %collective-permute-start.5 = (bf16[360,2048]{1,0:T(8,128)(2,1)}, bf16[360,2048]{1,0:T(8,128)(2,1)}, u32[]{:S(2)}, u32[]{:S(2)}) collective-permute-start(bf16[360,2048]{1,0:T(8,128)(2,1)} %get-tuple-element.13.kv0), channel_id=1, source_target_pairs={{0,1},{1,0},{2,3},{3,2},{4,5},{5,4},{6,7},{7,6},{8,9},{9,8},{10,11... | collective-permute-start | bytes 4423688 | tf_op jit(solution)/shard_map/ppermute | solution.py:40
  20.1 1.6 %relayout.1.value_ref = bf16[4,80,1536]{2,1,0:T(8,128)(2,1)} custom-call(bf16[76,4,1440]{2,1,0:T(4,128)(2,1)S(1)} %copy-done.12, s32[4,1440]{1,0:T(4,128)S(1)} %copy-done.16, bf16[360,1024]{1,0:T(8,128)(2,1)S(1)} %get-tuple-element.12.after_ref.q_ref), custom_call_target="tpu_custom_call" | custom-call | flops 999999995904 | bytes 1000000000 | tf_op jit(solution)/shard_map/relayout/pallas_call | solution.py:149
  21.7 0.0 collective-permute-start.2
  21.8 2.9 %collective-permute-start.3 = (bf16[4,80,1536]{2,1,0:T(8,128)(2,1)}, bf16[4,80,1536]{2,1,0:T(8,128)(2,1)}, u32[]{:S(2)}, u32[]{:S(2)}) collective-permute-start(bf16[4,80,1536]{2,1,0:T(8,128)(2,1)} %gate.1.x0), channel_id=1, source_target_pairs={{1,2},{2,1},{3,4},{4,3},{5,6},{6,5},{7,8},{8,7},{9,10},{10,9},{11,... | collective-permute-start | bytes 2949128 | tf_op jit(solution)/shard_map/ppermute | solution.py:48
  24.7 11.9 %near.1 = (f32[360,1024]{1,0:T(8,128)S(1)}, f32[360,1024]{1,0:T(8,128)S(1)}, f32[360,1024]{1,0:T(8,128)S(1)}) custom-call(bf16[360,1024]{1,0:T(8,128)(2,1)S(1)} %get-tuple-element.12.after_ref.q_ref, bf16[360,2048]{1,0:T(8,128)(2,1)} %get-tuple-element.13.kv0, bf16[360,2048]{1,0:T(8,128)(2,1)} %collective-permute-done.5.kv1), custom_call_target="tpu_custom_call" | custom-call | flops 1 | bytes 1 | tf_op jit(solution)/shard_map/near/pallas_call | solution.py:301
  36.6 5.0 %collective-permute-done.4.atmos_ref = bf16[360,1024]{1,0:T(8,128)(2,1)} collective-permute-done((bf16[360,1024]{1,0:T(8,128)(2,1)}, bf16[360,1024]{1,0:T(8,128)(2,1)}, u32[]{:S(2)}, u32[]{:S(2)}) %collective-permute-start.4) | collective-permute-done | bytes 737312 | tf_op jit(solution)/shard_map/ppermute | solution.py:48
  41.6 0.0 copy-start.1
  41.6 0.0 copy-start.10
  41.7 0.0 copy-start.19
  41.7 4.0 %project.3.kv_ref = bf16[360,2048]{1,0:T(8,128)(2,1)S(1)} custom-call(s32[1]{0:T(128)} %bitcast.pos_ref, f32[16]{0:T(128)S(1)} %copy-done.20, bf16[360,1024]{1,0:T(8,128)(2,1)} %collective-permute-done.4.atmos_ref, bf16[32,384]{1,0:T(8,128)(2,1)S(1)} %copy-done.7, bf16[32,384]{1,0:T(8,128)(2,1)S(1)} %surface.1.m0.after_ref.m1.p0, ...), custom_call_target="tpu_custom_call" | custom-call | flops 999999995904 | bytes 1000000000 | tf_op jit(solution)/shard_map/project/pallas_call | solution.py:243
  45.7 0.0 copy-start.3
  45.8 0.0 copy-start.13
  45.8 7.3 %far.1 = (bf16[360,1024]{1,0:T(8,128)(2,1)S(1)}, bf16[16,384]{1,0:T(8,128)(2,1)S(1)}) custom-call(bf16[32,384]{1,0:T(8,128)(2,1)S(1)} %copy-done.7, bf16[360,1024]{1,0:T(8,128)(2,1)S(1)} %copy-done.1, bf16[360,2048]{1,0:T(8,128)(2,1)S(1)} %project.3.kv_ref, f32[360,1024]{1,0:T(8,128)S(1)} %get-tuple-element.14.after_ref.top_ref, ...), custom_call_target="tpu_custom_call" | custom-call | flops 999999995904 | bytes 1000000000 | tf_op jit(solution)/shard_map/far/pallas_call | solution.py:349
  53.1 1.2 %collective-permute-done.6.f1 = bf16[16,384]{1,0:T(8,128)(2,1)S(1)} collective-permute-done((bf16[16,384]{1,0:T(8,128)(2,1)S(1)}, bf16[16,384]{1,0:T(8,128)(2,1)S(1)}, u32[]{:S(2)}, u32[]{:S(2)}) %collective-permute-start.6) | collective-permute-done | bytes 12320 | tf_op jit(solution)/shard_map/ppermute | solution.py:40
  54.3 2.1 %collective-permute-start.7 = (bf16[2,16,384]{2,1,0:T(8,128)(2,1)S(1)}, bf16[2,16,384]{2,1,0:T(8,128)(2,1)S(1)}, u32[]{:S(2)}, u32[]{:S(2)}) collective-permute-start(bf16[2,16,384]{2,1,0:T(8,128)(2,1)S(1)} %pad_maximum_fusion.1), channel_id=1, source_target_pairs={{1,2},{2,1},{3,4},{4,3},{5,6},{6,5},{7,8},{8,7},{9,10},{10,9},{11,... | collective-permute-start | bytes 73736 | tf_op jit(solution)/shard_map/ppermute | solution.py:48
  56.4 3.3 %collective-permute-done.7.fx = bf16[2,16,384]{2,1,0:T(8,128)(2,1)S(1)} collective-permute-done((bf16[2,16,384]{2,1,0:T(8,128)(2,1)S(1)}, bf16[2,16,384]{2,1,0:T(8,128)(2,1)S(1)}, u32[]{:S(2)}, u32[]{:S(2)}) %collective-permute-start.7) | collective-permute-done | bytes 24608 | tf_op jit(solution)/shard_map/ppermute | solution.py:48
  59.8 0.8 collective-permute-start.8
  60.5 0.8 %collective-permute-done.8.fy = bf16[2,16,384]{2,1,0:T(8,128)(2,1)S(1)} collective-permute-done((bf16[2,16,384]{2,1,0:T(8,128)(2,1)S(1)}, bf16[2,16,384]{2,1,0:T(8,128)(2,1)S(1)}, u32[]{:S(2)}, u32[]{:S(2)}) %collective-permute-start.8) | collective-permute-done | bytes 24608 | tf_op jit(solution)/shard_map/ppermute | solution.py:40
  61.4 17.7 %ocean.1 = (bf16[76,4,1440]{2,1,0:T(4,128)(2,1)}, bf16[360,1024]{1,0:T(8,128)(2,1)}) custom-call(s32[1]{0:T(128)} %bitcast.pos_ref, bf16[4,80,1536]{2,1,0:T(8,128)(2,1)} %gate.1.x0, bf16[4,80,1536]{2,1,0:T(8,128)(2,1)} %collective-permute-done.2.x1, bf16[4,80,1536]{2,1,0:T(8,128)(2,1)} %collective-permute-done.3.x2, bf16[32,384]{1,0:T(8,128)(2,1)S(1)} %copy-done.3, ...), custom_call_target="tpu_custom_call" | custom-call | flops 20000000000 | bytes 10000000 | tf_op jit(solution)/shard_map/ocean/pallas_call | solution.py:530
  (42 shorter events, 0.1 us)
Async XLA Ops:
  3.4 1.2 %copy-start.11 = (bf16[76,4,1440]{2,1,0:T(4,128)(2,1)S(1)}, bf16[76,4,1440]{2,1,0:T(4,128)(2,1)}, u32[]{:S(2)}) copy-start(bf16[76,4,1440]{2,1,0:T(4,128)(2,1)} %ocean_ref.3) | copy-start | bytes 2626564
  4.6 7.6 %copy-start.8 = (bf16[1024,3072]{1,0:T(8,128)(2,1)S(1)}, bf16[1024,3072]{1,0:T(8,128)(2,1)}, u32[]{:S(2)}) copy-start(bf16[1024,3072]{1,0:T(8,128)(2,1)} %w_ref.3) | copy-start | bytes 18874372
  4.6 7.6 %copy-start.17 = (f32[4,1024]{1,0:T(4,128)S(1)}, f32[4,1024]{1,0:T(4,128)}, u32[]{:S(2)}) copy-start(f32[4,1024]{1,0:T(4,128)} %embed_ref.3) | copy-start | bytes 49156
  4.6 7.6 %copy-start.18 = (f32[1024]{0:T(1024)S(1)}, f32[1024]{0:T(1024)}, u32[]{:S(2)}) copy-start(f32[1024]{0:T(1024)} %param.22) | copy-start | bytes 12292
  4.6 7.6 %copy-start.20 = (f32[16]{0:T(128)S(1)}, f32[16]{0:T(128)}, u32[]{:S(2)}) copy-start(f32[16]{0:T(128)} %scale_ref.3) | copy-start | bytes 196
  4.9 36.7 %copy-start.2 = (bf16[32,384]{1,0:T(8,128)(2,1)}, bf16[32,384]{1,0:T(8,128)(2,1)S(1)}, u32[]{:S(2)}) copy-start(bf16[32,384]{1,0:T(8,128)(2,1)S(1)} %surface.1.m0.after_ref.m1.p0) | copy-start | bytes 73732
  5.0 1.6 %collective-permute-start = (bf16[32,384]{1,0:T(8,128)(2,1)S(1)}, bf16[32,384]{1,0:T(8,128)(2,1)S(1)}, u32[]{:S(2)}, u32[]{:S(2)}) collective-permute-start(bf16[32,384]{1,0:T(8,128)(2,1)S(1)} %surface.1.m0.after_ref.m1.p0), channel_id=1, source_target_pairs={{0,1},{1,0},{2,3},{3,2},{4,5},{5,4},{6,7},{7,6},{8,9},{9,8},{10,11... | collective-permute-start | bytes 73736 | tf_op jit(solution)/shard_map/ppermute | solution.py:40
  6.5 12.1 %copy-start.4 = (bf16[32,384]{1,0:T(8,128)(2,1)}, bf16[32,384]{1,0:T(8,128)(2,1)S(1)}, u32[]{:S(2)}) copy-start(bf16[32,384]{1,0:T(8,128)(2,1)S(1)} %collective-permute-done.m1.p1) | copy-start | bytes 73732
  6.6 5.6 %collective-permute-start.1 = (bf16[2,32,384]{2,1,0:T(8,128)(2,1)S(1)}, bf16[2,32,384]{2,1,0:T(8,128)(2,1)S(1)}, u32[]{:S(2)}, u32[]{:S(2)}) collective-permute-start(bf16[2,32,384]{2,1,0:T(8,128)(2,1)S(1)} %pad_maximum_fusion), channel_id=1, source_target_pairs={{1,2},{2,1},{3,4},{4,3},{5,6},{6,5},{7,8},{8,7},{9,10},{10,9},{11,... | collective-permute-start | bytes 147464 | tf_op jit(solution)/shard_map/ppermute | solution.py:48
  10.1 31.5 %collective-permute-start.4 = (bf16[360,1024]{1,0:T(8,128)(2,1)}, bf16[360,1024]{1,0:T(8,128)(2,1)}, u32[]{:S(2)}, u32[]{:S(2)}) collective-permute-start(bf16[360,1024]{1,0:T(8,128)(2,1)} %atmos_ref.1), channel_id=1, source_target_pairs={{1,2},{2,1},{3,4},{4,3},{5,6},{6,5},{7,8},{8,7},{9,10},{10,9},{11,... | collective-permute-start | bytes 2211848 | tf_op jit(solution)/shard_map/ppermute | solution.py:48
  12.2 6.5 %copy-start.6 = (bf16[32,384]{1,0:T(8,128)(2,1)}, bf16[32,384]{1,0:T(8,128)(2,1)S(1)}, u32[]{:S(2)}) copy-start(bf16[32,384]{1,0:T(8,128)(2,1)S(1)} %get-tuple-element.23.m2.m0.message_ref.p2) | copy-start | bytes 73732
  12.2 7.9 %copy-start.12 = (bf16[76,4,1440]{2,1,0:T(4,128)(2,1)S(1)}, bf16[76,4,1440]{2,1,0:T(4,128)(2,1)}, u32[]{:S(2)}) copy-start(bf16[76,4,1440]{2,1,0:T(4,128)(2,1)} %ocean_ref.3) | copy-start | bytes 2626564
  12.2 7.9 %copy-start.16 = (s32[4,1440]{1,0:T(4,128)S(1)}, s32[4,1440]{1,0:T(4,128)}, u32[]{:S(2)}) copy-start(s32[4,1440]{1,0:T(4,128)} %mask_ref.1) | copy-start | bytes 69124
  18.7 6.0 %copy-start = (bf16[360,1024]{1,0:T(8,128)(2,1)}, bf16[360,1024]{1,0:T(8,128)(2,1)S(1)}, u32[]{:S(2)}) copy-start(bf16[360,1024]{1,0:T(8,128)(2,1)S(1)} %get-tuple-element.12.after_ref.q_ref) | copy-start | bytes 2211844
  18.7 6.0 %collective-permute-start.5 = (bf16[360,2048]{1,0:T(8,128)(2,1)}, bf16[360,2048]{1,0:T(8,128)(2,1)}, u32[]{:S(2)}, u32[]{:S(2)}) collective-permute-start(bf16[360,2048]{1,0:T(8,128)(2,1)} %get-tuple-element.13.kv0), channel_id=1, source_target_pairs={{0,1},{1,0},{2,3},{3,2},{4,5},{5,4},{6,7},{7,6},{8,9},{9,8},{10,11... | collective-permute-start | bytes 4423688 | tf_op jit(solution)/shard_map/ppermute | solution.py:40
  21.7 19.9 %copy-start.9 = (bf16[1024,3072]{1,0:T(8,128)(2,1)S(1)}, bf16[1024,3072]{1,0:T(8,128)(2,1)}, u32[]{:S(2)}) copy-start(bf16[1024,3072]{1,0:T(8,128)(2,1)} %w_ref.3) | copy-start | bytes 18874372
  21.7 19.9 %copy-start.7 = (bf16[32,384]{1,0:T(8,128)(2,1)S(1)}, bf16[32,384]{1,0:T(8,128)(2,1)}, u32[]{:S(2)}) copy-start(bf16[32,384]{1,0:T(8,128)(2,1)} %copy-done.6) | copy-start | bytes 73732
  21.7 38.8 %collective-permute-start.2 = (bf16[4,80,1536]{2,1,0:T(8,128)(2,1)}, bf16[4,80,1536]{2,1,0:T(8,128)(2,1)}, u32[]{:S(2)}, u32[]{:S(2)}) collective-permute-start(bf16[4,80,1536]{2,1,0:T(8,128)(2,1)} %gate.1.x0), channel_id=1, source_target_pairs={{0,1},{1,0},{2,3},{3,2},{4,5},{5,4},{6,7},{7,6},{8,9},{9,8},{10,11... | collective-permute-start | bytes 2949128 | tf_op jit(solution)/shard_map/ppermute | solution.py:40
  21.8 38.7 %collective-permute-start.3 = (bf16[4,80,1536]{2,1,0:T(8,128)(2,1)}, bf16[4,80,1536]{2,1,0:T(8,128)(2,1)}, u32[]{:S(2)}, u32[]{:S(2)}) collective-permute-start(bf16[4,80,1536]{2,1,0:T(8,128)(2,1)} %gate.1.x0), channel_id=1, source_target_pairs={{1,2},{2,1},{3,4},{4,3},{5,6},{6,5},{7,8},{8,7},{9,10},{10,9},{11,... | collective-permute-start | bytes 2949128 | tf_op jit(solution)/shard_map/ppermute | solution.py:48
  41.6 4.1 %copy-start.1 = (bf16[360,1024]{1,0:T(8,128)(2,1)S(1)}, bf16[360,1024]{1,0:T(8,128)(2,1)}, u32[]{:S(2)}) copy-start(bf16[360,1024]{1,0:T(8,128)(2,1)} %copy-done) | copy-start | bytes 2211844
  41.6 4.1 %copy-start.10 = (bf16[1024,1024]{1,0:T(8,128)(2,1)S(1)}, bf16[1024,1024]{1,0:T(8,128)(2,1)}, u32[]{:S(2)}) copy-start(bf16[1024,1024]{1,0:T(8,128)(2,1)} %wo_ref.1) | copy-start | bytes 6291460
  41.7 4.1 %copy-start.15 = (bf16[1024,16]{0,1:T(8,128)(2,1)S(1)}, bf16[1024,16]{0,1:T(8,128)(2,1)}, u32[]{:S(2)}) copy-start(bf16[1024,16]{0,1:T(8,128)(2,1)} %param.24) | copy-start | bytes 98308
  41.7 4.1 %copy-start.19 = (f32[1024]{0:T(1024)S(1)}, f32[1024]{0:T(1024)}, u32[]{:S(2)}) copy-start(f32[1024]{0:T(1024)} %param.23) | copy-start | bytes 12292
  45.7 15.6 %copy-start.3 = (bf16[32,384]{1,0:T(8,128)(2,1)S(1)}, bf16[32,384]{1,0:T(8,128)(2,1)}, u32[]{:S(2)}) copy-start(bf16[32,384]{1,0:T(8,128)(2,1)} %copy-done.2) | copy-start | bytes 73732
  45.8 15.6 %copy-start.5 = (bf16[32,384]{1,0:T(8,128)(2,1)S(1)}, bf16[32,384]{1,0:T(8,128)(2,1)}, u32[]{:S(2)}) copy-start(bf16[32,384]{1,0:T(8,128)(2,1)} %copy-done.4) | copy-start | bytes 73732
  45.8 15.6 %copy-start.13 = (bf16[9,128,92]{1,2,0:T(8,128)(2,1)S(1)}, bf16[9,128,92]{1,2,0:T(8,128)(2,1)}, u32[]{:S(2)}) copy-start(bf16[9,128,92]{1,2,0:T(8,128)(2,1)} %param.30) | copy-start | bytes 635908
  45.8 15.6 %copy-start.14 = (bf16[9,76,128]{2,1,0:T(8,128)(2,1)S(1)}, bf16[9,76,128]{2,1,0:T(8,128)(2,1)}, u32[]{:S(2)}) copy-start(bf16[9,76,128]{2,1,0:T(8,128)(2,1)} %c2_ref.1) | copy-start | bytes 525316
  53.1 1.2 %collective-permute-start.6 = (bf16[16,384]{1,0:T(8,128)(2,1)S(1)}, bf16[16,384]{1,0:T(8,128)(2,1)S(1)}, u32[]{:S(2)}, u32[]{:S(2)}) collective-permute-start(bf16[16,384]{1,0:T(8,128)(2,1)S(1)} %get-tuple-element.18.f0), channel_id=1, source_target_pairs={{0,1},{1,0},{2,3},{3,2},{4,5},{5,4},{6,7},{7,6},{8,9},{9,8},{10,11... | collective-permute-start | bytes 36872 | tf_op jit(solution)/shard_map/ppermute | solution.py:40
  54.3 5.4 %collective-permute-start.7 = (bf16[2,16,384]{2,1,0:T(8,128)(2,1)S(1)}, bf16[2,16,384]{2,1,0:T(8,128)(2,1)S(1)}, u32[]{:S(2)}, u32[]{:S(2)}) collective-permute-start(bf16[2,16,384]{2,1,0:T(8,128)(2,1)S(1)} %pad_maximum_fusion.1), channel_id=1, source_target_pairs={{1,2},{2,1},{3,4},{4,3},{5,6},{6,5},{7,8},{8,7},{9,10},{10,9},{11,... | collective-permute-start | bytes 73736 | tf_op jit(solution)/shard_map/ppermute | solution.py:48
  59.8 1.6 %collective-permute-start.8 = (bf16[2,16,384]{2,1,0:T(8,128)(2,1)S(1)}, bf16[2,16,384]{2,1,0:T(8,128)(2,1)S(1)}, u32[]{:S(2)}, u32[]{:S(2)}) collective-permute-start(bf16[2,16,384]{2,1,0:T(8,128)(2,1)S(1)} %collective-permute-done.7.fx), channel_id=1, source_target_pairs={{0,1},{1,0},{2,3},{3,2},{4,5},{5,4},{6,7},{7,6},{8,9},{9,8},{10,11... | collective-permute-start | bytes 73736 | tf_op jit(solution)/shard_map/ppermute | solution.py:40
